TPU v7x, 512 devices: a whole 4x8x8 slice. The times are simulated.
512 devices in a mesh: gx: 8 (over y_lo, core), gy: 8 (over y_hi, x), gz: 8 (over z).
Axes of the slice: x: 4, y: 8 (y_hi: 2, y_lo: 4; y = y_hi * 4 + y_lo), z: 8, core: 2. Of those that a mesh axis runs over, the one named last changes fastest.
Arguments:
- volume: bfloat16 [16, 32, 64, 1024], P(None, 'gx', 'gy', 'gz'), may hold values from -6 to 6
- enc_weight: bfloat16 [27, 16, 16], replicated, may hold values from -0.3125 to 0.3125
- coarse_weight: bfloat16 [27, 16, 32], replicated, may hold values from -0.3125 to 0.3125
- up_weight: bfloat16 [32, 16], replicated, may hold values from -1 to 1
- dec_weight: bfloat16 [27, 32, 16], replicated, may hold values from -0.21875 to 0.21875
- cotangent: bfloat16 [16, 32, 64, 1024], P(None, 'gx', 'gy', 'gz'), may hold values from -6 to 6
Outputs:
- decoded: bfloat16 [16, 32, 64, 1024], P(None, 'gx', 'gy', 'gz')
- volume_grad: bfloat16 [16, 32, 64, 1024], P(None, 'gx', 'gy', 'gz')
- enc_grad: float32 [27, 16, 16], replicated
- coarse_grad: float32 [27, 16, 32], replicated
- up_grad: float32 [32, 16], replicated
- dec_grad: float32 [27, 32, 16], replicated
All inputs are finite; a program needn't handle non-finite values.
Results may differ from a plain program's by a relative error of at most 0.013.
Values may be sent and summed in bfloat16 or wider, within the bound.
A program may use at most 64 MiB of HBM per device.

v0:
```python
import jax
import jax.numpy as jnp
from jax import lax
from jax.sharding import PartitionSpec as P


def extended(block, sides, width):
    for axis, dim in sides:
        count = lax.axis_size(axis)
        forward = [(i, i + 1) for i in range(count - 1)]
        backward = [(target, source) for source, target in forward]
        low = lax.ppermute(
            lax.slice_in_dim(block, block.shape[dim] - width, None, axis=dim), axis, forward
        )
        high = lax.ppermute(lax.slice_in_dim(block, 0, width, axis=dim), axis, backward)
        block = jnp.concatenate([low, block, high], axis=dim)
    return block


def packed_total(arrays, axis):
    ends = [0]
    for a in arrays:
        ends.append(ends[-1] + a.size)
    total = lax.psum(jnp.concatenate([a.ravel() for a in arrays]), axis)
    return tuple((total[b:e].reshape(a.shape) for a, b, e in zip(arrays, ends, ends[1:])))


def convolve(padded, weight):
    chans = padded.shape[0]
    depth = padded.shape[1] - 2
    height = padded.shape[2] - 2
    width = padded.shape[3] - 2
    outputs = weight.shape[2]
    total = jnp.zeros((outputs, depth, height, width), jnp.float32)
    for a in range(3):
        for b in range(3):
            stacked = jnp.concatenate(
                [padded[:, a : a + depth, b : b + height, c : c + width] for c in range(3)], axis=0
            )
            first = (a * 3 + b) * 3
            kernel = weight[first : first + 3].reshape(3 * chans, outputs)
            total = total + jnp.einsum(
                "ko,kxyz->oxyz", kernel, stacked, preferred_element_type=jnp.float32
            )
    return total


def weight_grad(padded, grad_out):
    chans = padded.shape[0]
    depth = grad_out.shape[1]
    height = grad_out.shape[2]
    width = grad_out.shape[3]
    outputs = grad_out.shape[0]
    pieces = []
    for a in range(3):
        for b in range(3):
            stacked = jnp.concatenate(
                [padded[:, a : a + depth, b : b + height, c : c + width] for c in range(3)], axis=0
            )
            part = jnp.einsum(
                "kxyz,oxyz->ko", stacked, grad_out, preferred_element_type=jnp.float32
            )
            pieces.append(part.reshape(3, chans, outputs))
    return jnp.concatenate(pieces, axis=0)


def flipped(weight):
    return jnp.transpose(weight[::-1], (0, 2, 1))


def silu_slope(value):
    sig = jax.nn.sigmoid(value)
    return sig * (1.0 + value * (1.0 - sig))


def block_sum(field):
    chans, depth, height, width = field.shape
    return field.reshape(chans, depth // 2, 2, height // 2, 2, width // 2, 2).sum(axis=(2, 4, 6))


def enlarge(field):
    return jnp.repeat(jnp.repeat(jnp.repeat(field, 2, axis=1), 2, axis=2), 2, axis=3)


def per_device(volume, enc_weight, coarse_weight, up_weight, dec_weight, cotangent):
    chans, depth, height, width = volume.shape
    joint = jnp.concatenate([volume, cotangent], axis=0)
    rimmed = extended(joint, (("gx", 1), ("gy", 2), ("gz", 3)), 1)
    vol_rim = rimmed[:chans]
    cot_rim = rimmed[chans:]
    pre_enc = convolve(vol_rim, enc_weight)
    skip = jax.nn.silu(pre_enc).astype(jnp.bfloat16)
    skip_rim = extended(skip, (("gx", 1), ("gy", 2), ("gz", 3)), 1)
    pooled = (block_sum(skip.astype(jnp.float32)) * 0.125).astype(jnp.bfloat16)
    pooled_rim = extended(pooled, (("gx", 1), ("gy", 2), ("gz", 3)), 1)
    pre_coarse = convolve(pooled_rim, coarse_weight)
    coarse_act = jax.nn.silu(pre_coarse).astype(jnp.bfloat16)
    upper = jnp.einsum(
        "io,ixyz->oxyz", up_weight, coarse_act, preferred_element_type=jnp.float32
    ).astype(jnp.bfloat16)
    upper_rim = extended(upper, (("gx", 1), ("gy", 2), ("gz", 3)), 1)
    up_rim = enlarge(upper_rim)[:, 1:-1, 1:-1, 1:-1]
    joined_rim = jnp.concatenate([skip_rim, up_rim], axis=0)
    decoded = convolve(joined_rim, dec_weight).astype(jnp.bfloat16)
    dec_local = weight_grad(joined_rim, cotangent)
    joined_grad = convolve(cot_rim, flipped(dec_weight))
    upper_grad = block_sum(joined_grad[chans:]).astype(jnp.bfloat16)
    up_local = jnp.einsum(
        "ixyz,oxyz->io", coarse_act, upper_grad, preferred_element_type=jnp.float32
    )
    act_grad = jnp.einsum(
        "io,oxyz->ixyz", up_weight, upper_grad, preferred_element_type=jnp.float32
    )
    coarse_pre_grad = (act_grad * silu_slope(pre_coarse)).astype(jnp.bfloat16)
    coarse_local = weight_grad(pooled_rim, coarse_pre_grad)
    coarse_rim = extended(coarse_pre_grad, (("gx", 1), ("gy", 2), ("gz", 3)), 1)
    pooled_grad = convolve(coarse_rim, flipped(coarse_weight))
    skip_grad = joined_grad[:chans] + enlarge(pooled_grad) * 0.125
    enc_pre_grad = (skip_grad * silu_slope(pre_enc)).astype(jnp.bfloat16)
    enc_local = weight_grad(vol_rim, enc_pre_grad)
    enc_rim = extended(enc_pre_grad, (("gx", 1), ("gy", 2), ("gz", 3)), 1)
    volume_grad = convolve(enc_rim, flipped(enc_weight)).astype(jnp.bfloat16)
    enc_grad, coarse_grad, up_grad, dec_grad = packed_total(
        (enc_local, coarse_local, up_local, dec_local), ("gx", "gy", "gz")
    )
    return (decoded, volume_grad, enc_grad, coarse_grad, up_grad, dec_grad)


def solution(mesh):
    return jax.shard_map(
        per_device,
        mesh=mesh,
        in_specs=(P(None, "gx", "gy", "gz"), P(), P(), P(), P(), P(None, "gx", "gy", "gz")),
        out_specs=(P(None, "gx", "gy", "gz"), P(None, "gx", "gy", "gz"), P(), P(), P(), P()),
        check_vma=False,
    )
```

profile of v0, /device:TPU:1, one launch (start us, length us, event | category | flops | bytes accessed | tf_op | source)
XLA Modules:
  0.0 548.4 jit_solution(8037383385524209315)
XLA Ops:
  9.9 4.6 collective-permute-start
  14.5 5.5 %collective-permute-start.1 = (bf16[32,1,8,128]{3,0,2,1:T(8,128)(2,1)S(1)}, bf16[32,1,8,128]{3,0,2,1:T(8,128)(2,1)S(1)}, u32[]{:S(2)}, u32[]{:S(2)}) collective-permute-start(bf16[32,1,8,128]{3,0,2,1:T(8,128)(2,1)S(1)} %get-tuple-element.132), channel_id=1, source_target_pairs={{64,0},{128,64},{192,128},{256,192},{320,256},{384,320},{448,384},... | collective-permute-start | bytes 196616 | tf_op jit(solution)/shard_map/ppermute | solution.py:15
  53.8 7.3 %collective-permute-done.4 = bf16[32,6,10,1]{3,0,2,1:T(8,128)(2,1)S(1)} collective-permute-done((bf16[32,6,10,1]{3,0,2,1:T(8,128)(2,1)S(1)}, bf16[32,6,10,1]{3,0,2,1:T(8,128)(2,1)S(1)}, u32[]{:S(2)}, u32[]{:S(2)}) %collective-permute-start.4) | collective-permute-done | bytes 3872 | tf_op jit(solution)/shard_map/ppermute | solution.py:12
  61.1 4.5 collective-permute-done.5
  74.1 5.0 collective-permute-start.6
  82.6 3.6 collective-permute-start.12
  94.2 4.6 collective-permute-start.14
  104.4 4.0 collective-permute-start.16
  111.0 6.0 %collective-permute-done.17 = bf16[16,4,6,1]{3,0,2,1:T(8,128)(2,1)S(1)} collective-permute-done((bf16[16,4,6,1]{3,0,2,1:T(8,128)(2,1)S(1)}, bf16[16,4,6,1]{3,0,2,1:T(8,128)(2,1)S(1)}, u32[]{:S(2)}, u32[]{:S(2)}) %collective-permute-start.17) | collective-permute-done | bytes 800 | tf_op jit(solution)/shard_map/ppermute | solution.py:15
  122.4 4.9 collective-permute-start.18
  129.2 3.6 collective-permute-start.24
  136.0 3.9 collective-permute-start.20
  142.6 10.6 %collective-permute-start.8 = (bf16[16,6,1,128]{3,0,2,1:T(8,128)(2,1)}, bf16[16,6,1,128]{3,0,2,1:T(8,128)(2,1)}, u32[]{:S(2)}, u32[]{:S(2)}) collective-permute-start(bf16[16,6,1,128]{3,0,2,1:T(8,128)(2,1)} %get-tuple-element.171), channel_id=1, source_target_pairs={{0,8},{8,16},{16,24},{24,32},{32,40},{40,48},{48,56},{1,9},{9,17},... | collective-permute-start | bytes 73736 | tf_op jit(solution)/shard_map/ppermute | solution.py:12
  154.6 4.6 collective-permute-start.22
  161.2 10.4 %collective-permute-start.26 = (bf16[32,4,1,64]{3,0,2,1:T(8,128)(2,1)}, bf16[32,4,1,64]{3,0,2,1:T(8,128)(2,1)}, u32[]{:S(2)}, u32[]{:S(2)}) collective-permute-start(bf16[32,4,1,64]{3,0,2,1:T(8,128)(2,1)} %get-tuple-element.185), channel_id=1, source_target_pairs={{0,8},{8,16},{16,24},{24,32},{32,40},{40,48},{48,56},{1,9},{9,17},... | collective-permute-start | bytes 49160 | tf_op jit(solution)/shard_map/ppermute | solution.py:12
  179.0 4.3 collective-permute-start.28
  187.7 4.3 collective-permute-done.29
  211.1 4.6 collective-permute-start.30
  235.9 4.3 concatenate.527
  246.0 7.8 %collective-permute-start.32 = (bf16[16,6,1,128]{3,0,2,1:T(8,128)(2,1)S(1)}, bf16[16,6,1,128]{3,0,2,1:T(8,128)(2,1)S(1)}, u32[]{:S(2)}, u32[]{:S(2)}) collective-permute-start(bf16[16,6,1,128]{3,0,2,1:T(8,128)(2,1)S(1)} %get-tuple-element.147), channel_id=1, source_target_pairs={{0,8},{8,16},{16,24},{24,32},{32,40},{40,48},{48,56},{1,9},{9,17},... | collective-permute-start | bytes 73736 | tf_op jit(solution)/shard_map/ppermute | solution.py:12
  256.1 8.6 %collective-permute-done.33 = bf16[16,6,1,128]{3,0,2,1:T(8,128)(2,1)S(1)} collective-permute-done((bf16[16,6,1,128]{3,0,2,1:T(8,128)(2,1)S(1)}, bf16[16,6,1,128]{3,0,2,1:T(8,128)(2,1)S(1)}, u32[]{:S(2)}, u32[]{:S(2)}) %collective-permute-start.33) | collective-permute-done | bytes 24608 | tf_op jit(solution)/shard_map/ppermute | solution.py:15
  264.9 4.3 collective-permute-start.34
  274.2 4.1 collective-permute-done.35
  282.1 253.5 %all-reduce.2.cloned.1.call-done = f32[35072]{0:T(1024)} async-done(((f32[35072]{0:T(1024)}), f32[35072]{0:T(1024)}) %all-reduce.2.cloned.1.call-update) | async-done | bytes 140304 | tf_op jit(solution)/shard_map/psum | solution.py:24
  (619 shorter events, 152.9 us)
Async XLA Ops:
  7.2 528.4 %all-reduce.2.cloned.1.call-start = ((), (), s32[]{:S(2)}) async-start(), calls=%async_computation | async-start | bytes 286720 | tf_op jit(solution)/shard_map/psum | solution.py:24
  9.9 13.9 %collective-permute-start = (bf16[32,1,8,128]{3,0,2,1:T(8,128)(2,1)S(1)}, bf16[32,1,8,128]{3,0,2,1:T(8,128)(2,1)S(1)}, u32[]{:S(2)}, u32[]{:S(2)}) collective-permute-start(bf16[32,1,8,128]{3,0,2,1:T(8,128)(2,1)S(1)} %get-tuple-element.131), channel_id=1, source_target_pairs={{0,64},{64,128},{128,192},{192,256},{256,320},{320,384},{384,448},... | collective-permute-start | bytes 196616 | tf_op jit(solution)/shard_map/ppermute | solution.py:12
  23.9 24.8 %collective-permute-start.2 = (bf16[32,6,1,128]{3,0,2,1:T(8,128)(2,1)S(1)}, bf16[32,6,1,128]{3,0,2,1:T(8,128)(2,1)S(1)}, u32[]{:S(2)}, u32[]{:S(2)}) collective-permute-start(bf16[32,6,1,128]{3,0,2,1:T(8,128)(2,1)S(1)} %get-tuple-element.129), channel_id=1, source_target_pairs={{0,8},{8,16},{16,24},{24,32},{32,40},{40,48},{48,56},{1,9},{9,17},... | collective-permute-start | bytes 147464 | tf_op jit(solution)/shard_map/ppermute | solution.py:12
  25.2 23.5 %collective-permute-start.3 = (bf16[32,6,1,128]{3,0,2,1:T(8,128)(2,1)S(1)}, bf16[32,6,1,128]{3,0,2,1:T(8,128)(2,1)S(1)}, u32[]{:S(2)}, u32[]{:S(2)}) collective-permute-start(bf16[32,6,1,128]{3,0,2,1:T(8,128)(2,1)S(1)} %get-tuple-element.130), channel_id=1, source_target_pairs={{8,0},{16,8},{24,16},{32,24},{40,32},{48,40},{56,48},{9,1},{17,9},... | collective-permute-start | bytes 147464 | tf_op jit(solution)/shard_map/ppermute | solution.py:15
  49.1 12.1 %collective-permute-start.4 = (bf16[32,6,10,1]{3,0,2,1:T(8,128)(2,1)S(1)}, bf16[32,6,10,1]{3,0,2,1:T(8,128)(2,1)S(1)}, u32[]{:S(2)}, u32[]{:S(2)}) collective-permute-start(bf16[32,6,10,1]{3,0,2,1:T(8,128)(2,1)S(1)} %get-tuple-element.113), channel_id=1, source_target_pairs={{0,1},{1,2},{2,3},{3,4},{4,5},{5,6},{6,7},{8,9},{9,10},{10,11},{11... | collective-permute-start | bytes 11528 | tf_op jit(solution)/shard_map/ppermute | solution.py:12
  51.4 14.2 %collective-permute-start.5 = (bf16[32,6,10,1]{3,0,2,1:T(8,128)(2,1)S(1)}, bf16[32,6,10,1]{3,0,2,1:T(8,128)(2,1)S(1)}, u32[]{:S(2)}, u32[]{:S(2)}) collective-permute-start(bf16[32,6,10,1]{3,0,2,1:T(8,128)(2,1)S(1)} %get-tuple-element.114), channel_id=1, source_target_pairs={{1,0},{2,1},{3,2},{4,3},{5,4},{6,5},{7,6},{9,8},{10,9},{11,10},{12... | collective-permute-start | bytes 11528 | tf_op jit(solution)/shard_map/ppermute | solution.py:15
  74.1 65.8 %collective-permute-start.6 = (bf16[16,1,8,128]{3,0,2,1:T(8,128)(2,1)}, bf16[16,1,8,128]{3,0,2,1:T(8,128)(2,1)}, u32[]{:S(2)}, u32[]{:S(2)}) collective-permute-start(bf16[16,1,8,128]{3,0,2,1:T(8,128)(2,1)} %get-tuple-element.189), channel_id=1, source_target_pairs={{0,64},{64,128},{128,192},{192,256},{256,320},{320,384},{384,448},... | collective-permute-start | bytes 98312 | tf_op jit(solution)/shard_map/ppermute | solution.py:12
  79.2 62.1 %collective-permute-start.7 = (bf16[16,1,8,128]{3,0,2,1:T(8,128)(2,1)}, bf16[16,1,8,128]{3,0,2,1:T(8,128)(2,1)}, u32[]{:S(2)}, u32[]{:S(2)}) collective-permute-start(bf16[16,1,8,128]{3,0,2,1:T(8,128)(2,1)} %get-tuple-element.190), channel_id=1, source_target_pairs={{64,0},{128,64},{192,128},{256,192},{320,256},{384,320},{448,384},... | collective-permute-start | bytes 98312 | tf_op jit(solution)/shard_map/ppermute | solution.py:15
  82.6 10.9 %collective-permute-start.12 = (bf16[16,1,4,64]{3,0,2,1:T(8,128)(2,1)S(1)}, bf16[16,1,4,64]{3,0,2,1:T(8,128)(2,1)S(1)}, u32[]{:S(2)}, u32[]{:S(2)}) collective-permute-start(bf16[16,1,4,64]{3,0,2,1:T(8,128)(2,1)S(1)} %get-tuple-element.287), channel_id=1, source_target_pairs={{0,64},{64,128},{128,192},{192,256},{256,320},{320,384},{384,448},... | collective-permute-start | bytes 24584 | tf_op jit(solution)/shard_map/ppermute | solution.py:12
  122.4 11.6 %collective-permute-start.18 = (bf16[16,1,4,64]{3,0,2,1:T(8,128)(2,1)S(1)}, bf16[16,1,4,64]{3,0,2,1:T(8,128)(2,1)S(1)}, u32[]{:S(2)}, u32[]{:S(2)}) collective-permute-start(bf16[16,1,4,64]{3,0,2,1:T(8,128)(2,1)S(1)} %get-tuple-element.285), channel_id=1, source_target_pairs={{0,64},{64,128},{128,192},{192,256},{256,320},{320,384},{384,448},... | collective-permute-start | bytes 24584 | tf_op jit(solution)/shard_map/ppermute | solution.py:12
  129.2 30.0 %collective-permute-start.24 = (bf16[32,1,4,64]{3,0,2,1:T(8,128)(2,1)S(1)}, bf16[32,1,4,64]{3,0,2,1:T(8,128)(2,1)S(1)}, u32[]{:S(2)}, u32[]{:S(2)}) collective-permute-start(bf16[32,1,4,64]{3,0,2,1:T(8,128)(2,1)S(1)} %get-tuple-element.268), channel_id=1, source_target_pairs={{0,64},{64,128},{128,192},{192,256},{256,320},{320,384},{384,448},... | collective-permute-start | bytes 49160 | tf_op jit(solution)/shard_map/ppermute | solution.py:12
  134.0 26.5 %collective-permute-start.25 = (bf16[32,1,4,64]{3,0,2,1:T(8,128)(2,1)S(1)}, bf16[32,1,4,64]{3,0,2,1:T(8,128)(2,1)S(1)}, u32[]{:S(2)}, u32[]{:S(2)}) collective-permute-start(bf16[32,1,4,64]{3,0,2,1:T(8,128)(2,1)S(1)} %get-tuple-element.269), channel_id=1, source_target_pairs={{64,0},{128,64},{192,128},{256,192},{320,256},{384,320},{448,384},... | collective-permute-start | bytes 49160 | tf_op jit(solution)/shard_map/ppermute | solution.py:15
  136.0 17.2 %collective-permute-start.20 = (bf16[16,4,1,64]{3,0,2,1:T(8,128)(2,1)S(1)}, bf16[16,4,1,64]{3,0,2,1:T(8,128)(2,1)S(1)}, u32[]{:S(2)}, u32[]{:S(2)}) collective-permute-start(bf16[16,4,1,64]{3,0,2,1:T(8,128)(2,1)S(1)} %get-tuple-element.270), channel_id=1, source_target_pairs={{0,8},{8,16},{16,24},{24,32},{32,40},{40,48},{48,56},{1,9},{9,17},... | collective-permute-start | bytes 24584 | tf_op jit(solution)/shard_map/ppermute | solution.py:12
  139.9 14.5 %collective-permute-start.21 = (bf16[16,4,1,64]{3,0,2,1:T(8,128)(2,1)S(1)}, bf16[16,4,1,64]{3,0,2,1:T(8,128)(2,1)S(1)}, u32[]{:S(2)}, u32[]{:S(2)}) collective-permute-start(bf16[16,4,1,64]{3,0,2,1:T(8,128)(2,1)S(1)} %get-tuple-element.271), channel_id=1, source_target_pairs={{8,0},{16,8},{24,16},{32,24},{40,32},{48,40},{56,48},{9,1},{17,9},... | collective-permute-start | bytes 24584 | tf_op jit(solution)/shard_map/ppermute | solution.py:15
  142.6 60.7 %collective-permute-start.8 = (bf16[16,6,1,128]{3,0,2,1:T(8,128)(2,1)}, bf16[16,6,1,128]{3,0,2,1:T(8,128)(2,1)}, u32[]{:S(2)}, u32[]{:S(2)}) collective-permute-start(bf16[16,6,1,128]{3,0,2,1:T(8,128)(2,1)} %get-tuple-element.171), channel_id=1, source_target_pairs={{0,8},{8,16},{16,24},{24,32},{32,40},{40,48},{48,56},{1,9},{9,17},... | collective-permute-start | bytes 73736 | tf_op jit(solution)/shard_map/ppermute | solution.py:12
  153.2 50.1 %collective-permute-start.9 = (bf16[16,6,1,128]{3,0,2,1:T(8,128)(2,1)}, bf16[16,6,1,128]{3,0,2,1:T(8,128)(2,1)}, u32[]{:S(2)}, u32[]{:S(2)}) collective-permute-start(bf16[16,6,1,128]{3,0,2,1:T(8,128)(2,1)} %get-tuple-element.172), channel_id=1, source_target_pairs={{8,0},{16,8},{24,16},{32,24},{40,32},{48,40},{56,48},{9,1},{17,9},... | collective-permute-start | bytes 73736 | tf_op jit(solution)/shard_map/ppermute | solution.py:15
  154.6 17.0 %collective-permute-start.22 = (bf16[16,4,6,1]{3,0,2,1:T(8,128)(2,1)S(1)}, bf16[16,4,6,1]{3,0,2,1:T(8,128)(2,1)S(1)}, u32[]{:S(2)}, u32[]{:S(2)}) collective-permute-start(bf16[16,4,6,1]{3,0,2,1:T(8,128)(2,1)S(1)} %get-tuple-element.229), channel_id=1, source_target_pairs={{0,1},{1,2},{2,3},{3,4},{4,5},{5,6},{6,7},{8,9},{9,10},{10,11},{11... | collective-permute-start | bytes 2312 | tf_op jit(solution)/shard_map/ppermute | solution.py:12
  159.2 13.7 %collective-permute-start.23 = (bf16[16,4,6,1]{3,0,2,1:T(8,128)(2,1)S(1)}, bf16[16,4,6,1]{3,0,2,1:T(8,128)(2,1)S(1)}, u32[]{:S(2)}, u32[]{:S(2)}) collective-permute-start(bf16[16,4,6,1]{3,0,2,1:T(8,128)(2,1)S(1)} %get-tuple-element.230), channel_id=1, source_target_pairs={{1,0},{2,1},{3,2},{4,3},{5,4},{6,5},{7,6},{9,8},{10,9},{11,10},{12... | collective-permute-start | bytes 2312 | tf_op jit(solution)/shard_map/ppermute | solution.py:15
  161.2 16.8 %collective-permute-start.26 = (bf16[32,4,1,64]{3,0,2,1:T(8,128)(2,1)}, bf16[32,4,1,64]{3,0,2,1:T(8,128)(2,1)}, u32[]{:S(2)}, u32[]{:S(2)}) collective-permute-start(bf16[32,4,1,64]{3,0,2,1:T(8,128)(2,1)} %get-tuple-element.185), channel_id=1, source_target_pairs={{0,8},{8,16},{16,24},{24,32},{32,40},{40,48},{48,56},{1,9},{9,17},... | collective-permute-start | bytes 49160 | tf_op jit(solution)/shard_map/ppermute | solution.py:12
  204.3 13.4 %collective-permute-start.10 = (bf16[16,6,10,1]{3,0,2,1:T(8,128)(2,1)S(1)}, bf16[16,6,10,1]{3,0,2,1:T(8,128)(2,1)S(1)}, u32[]{:S(2)}, u32[]{:S(2)}) collective-permute-start(bf16[16,6,10,1]{3,0,2,1:T(8,128)(2,1)S(1)} %get-tuple-element.137), channel_id=1, source_target_pairs={{0,1},{1,2},{2,3},{3,4},{4,5},{5,6},{6,7},{8,9},{9,10},{10,11},{11... | collective-permute-start | bytes 5768 | tf_op jit(solution)/shard_map/ppermute | solution.py:12
  207.4 10.2 %collective-permute-start.11 = (bf16[16,6,10,1]{3,0,2,1:T(8,128)(2,1)S(1)}, bf16[16,6,10,1]{3,0,2,1:T(8,128)(2,1)S(1)}, u32[]{:S(2)}, u32[]{:S(2)}) collective-permute-start(bf16[16,6,10,1]{3,0,2,1:T(8,128)(2,1)S(1)} %get-tuple-element.138), channel_id=1, source_target_pairs={{1,0},{2,1},{3,2},{4,3},{5,4},{6,5},{7,6},{9,8},{10,9},{11,10},{12... | collective-permute-start | bytes 5768 | tf_op jit(solution)/shard_map/ppermute | solution.py:15
  211.1 34.9 %collective-permute-start.30 = (bf16[16,1,8,128]{3,0,2,1:T(8,128)(2,1)}, bf16[16,1,8,128]{3,0,2,1:T(8,128)(2,1)S(1)}, u32[]{:S(2)}, u32[]{:S(2)}) collective-permute-start(bf16[16,1,8,128]{3,0,2,1:T(8,128)(2,1)} %get-tuple-element.181), channel_id=1, source_target_pairs={{0,64},{64,128},{128,192},{192,256},{256,320},{320,384},{384,448},... | collective-permute-start | bytes 98312 | tf_op jit(solution)/shard_map/ppermute | solution.py:12
  215.7 30.2 %collective-permute-start.31 = (bf16[16,1,8,128]{3,0,2,1:T(8,128)(2,1)}, bf16[16,1,8,128]{3,0,2,1:T(8,128)(2,1)S(1)}, u32[]{:S(2)}, u32[]{:S(2)}) collective-permute-start(bf16[16,1,8,128]{3,0,2,1:T(8,128)(2,1)} %get-tuple-element.182), channel_id=1, source_target_pairs={{64,0},{128,64},{192,128},{256,192},{320,256},{384,320},{448,384},... | collective-permute-start | bytes 98312 | tf_op jit(solution)/shard_map/ppermute | solution.py:15
  253.8 10.9 %collective-permute-start.33 = (bf16[16,6,1,128]{3,0,2,1:T(8,128)(2,1)S(1)}, bf16[16,6,1,128]{3,0,2,1:T(8,128)(2,1)S(1)}, u32[]{:S(2)}, u32[]{:S(2)}) collective-permute-start(bf16[16,6,1,128]{3,0,2,1:T(8,128)(2,1)S(1)} %get-tuple-element.148), channel_id=1, source_target_pairs={{8,0},{16,8},{24,16},{32,24},{40,32},{48,40},{56,48},{9,1},{17,9},... | collective-permute-start | bytes 73736 | tf_op jit(solution)/shard_map/ppermute | solution.py:15
  (154 other events, 1180.9 us)
Sparse Core Ops, SparseCore 0:
  256.2 279.3 all-reduce.1
where the time goes:
time: 551 us; the launch traced here: 548 us
  waiting for transfers between devices  294 us (53%)
  starting transfers between devices  119 us (22%)
  local copies, waits for them, and re-layouts  74 us (13%)
  matrix products  27.5 us (5%)
  other arithmetic  17.2 us (3%)
  between operations  16.6 us (3%)
    psum x1, waiting for transfers between devices, packed_total(): total = lax.psum(jnp.concatenate([a.ravel() for a in arrays]), axis)  253 us
    ppermute x18, starting transfers between devices, extended(): lax.ppermute(lax.slice_in_dim(block, block.shape[dim] - width, None, axis...  87.7 us
    ppermute x18, starting transfers between devices, extended(): lax.ppermute(lax.slice_in_dim(block, 0, width, axis=dim), axis, backward)  31.2 us
    ppermute x18, waiting for transfers between devices, extended(): lax.ppermute(lax.slice_in_dim(block, 0, width, axis=dim), axis, backward)  27.9 us
    reshape x36, local copies, waits for them, and re-layouts, convolve(): kernel = weight[first:first + 3].reshape(3 * chans, outputs)  18.2 us
    dot_general x54, matrix products, convolve(): jnp.einsum('ko,kxyz->oxyz', kernel, stacked, preferred_element_type=jnp.f...  15.8 us
    unnamed x298, local copies, waits for them, and re-layouts  13.9 us
    ppermute x18, waiting for transfers between devices, extended(): lax.ppermute(lax.slice_in_dim(block, block.shape[dim] - width, None, axis...  12.9 us
  transfers between devices with their start and end apart: 37, of which 11 were waited for; matrix products, arithmetic and copies ran while one was open for 18% of the time, Pallas kernels for 0%

commit v1 on v0

v1 whole, which is shorter than its diff:
```python
import functools

import jax
import jax.numpy as jnp
from jax import lax
from jax.experimental import pallas as pl
from jax.experimental.pallas import tpu as pltpu
from jax.sharding import PartitionSpec as P

AXES = ("gx", "gy", "gz")
BF = jnp.bfloat16
F32 = jnp.float32
MESH = pl.DeviceIdType.MESH
DIRS = tuple((dx, dy) for dx in (-1, 0, 1) for dy in (-1, 0, 1) if (dx, dy) != (0, 0))


def dot(a, b):
    return jnp.dot(a, b, preferred_element_type=F32)


def dot_nt(a, b):
    return lax.dot_general(a, b, (((1,), (1,)), ((), ())), preferred_element_type=F32)


def all_of(*conds):
    total = None
    for c in conds:
        if c is not None:
            total = c if total is None else jnp.logical_and(total, c)
    return total


def span(step, size, halo):
    if step == 0:
        return (0, size), (halo, size)
    if step > 0:
        return (size - halo, halo), (0, halo)
    return (0, halo), (halo + size, halo)


def kernel(sizes, vol, cot, we, wd, wdb, wc, wcb, web, upt, up, dec_out, vg_out, sum_out,
           vt, ct, pk, lr, vs, cs, skip, slope, jg, ughi, uglo, ug, ps, act, uc, gs, js, eh, es,
           gr, rx, ry, rz, ag,
           vsend, vrecv, csend, crecv, zsend, zrecv, lsend, lrecv, usend, urecv, esend, erecv,
           asend, arecv):
    nx, ny, nz = sizes
    ix, iy, iz = (lax.axis_index(a) for a in AXES)
    depth, height, chans, width = vol.shape
    cd, ch = depth // 2, height // 2

    def exists(step, index, count):
        return None if step == 0 else (index + step < count if step > 0 else index + step >= 0)

    def at(dx, dy, dz=0):
        return (ix + dx, iy + dy, iz + dz)

    def guarded(cond, f):
        if cond is None:
            f()
        else:
            pl.when(cond)(f)

    sends = [all_of(exists(dx, ix, nx), exists(dy, iy, ny)) for dx, dy in DIRS]
    recvs = [all_of(exists(-dx, ix, nx), exists(-dy, iy, ny)) for dx, dy in DIRS]
    zsteps = (-1, 1)
    zsends = [exists(s, iz, nz) for s in zsteps]
    zrecvs = [exists(-s, iz, nz) for s in zsteps]

    for ref in (vt, ct, lr, uc, eh):
        ref[...] = jnp.zeros(ref.shape, ref.dtype)
    barrier = pltpu.get_barrier_semaphore()

    def greet(device):
        pl.semaphore_signal(barrier, inc=1, device_id=device, device_id_type=MESH)

    for k in range(1, nx):
        greet((lax.rem(ix + k, nx), iy, iz))
    for k in range(1, ny):
        greet((ix, lax.rem(iy + k, ny), iz))
    for k in range(1, nz):
        greet((ix, iy, lax.rem(iz + k, nz)))
    for (dx, dy), s in zip(DIRS, sends):
        if dx != 0 and dy != 0:
            guarded(s, lambda dx=dx, dy=dy: greet(at(dx, dy)))
    def both(index, count):
        return (jnp.where(index > 0, 1, 0) + jnp.where(index < count - 1, 1, 0)).astype(jnp.int32)

    pl.semaphore_wait(barrier, nx + ny + nz - 3 + both(ix, nx) * both(iy, ny))

    def exchange(src, src_at, dst, dst_at, send_sem, recv_sem):
        copies = []
        for d, (dx, dy) in enumerate(DIRS):
            copies.append(pltpu.make_async_remote_copy(
                src_ref=src.at[src_at(dx, dy)], dst_ref=dst.at[dst_at(dx, dy)],
                send_sem=send_sem.at[d], recv_sem=recv_sem.at[d],
                device_id=at(dx, dy), device_id_type=MESH))
        return copies

    def begin(copies, conds):
        for c, s in zip(copies, conds):
            guarded(s, c.start)

    def landed(copies, conds):
        for c, r in zip(copies, conds):
            guarded(r, c.wait_recv)

    def left(copies, conds):
        for c, s in zip(copies, conds):
            guarded(s, c.wait_send)

    def rim_src(halo, d0, h0, off):
        def f(dx, dy):
            (a, n), _ = span(dx, d0, halo)
            (b, m), _ = span(dy, h0, halo)
            return (pl.ds(a + off, n), pl.ds(b + off, m))
        return f

    def rim_dst(halo, d0, h0):
        def f(dx, dy):
            _, (a, n) = span(dx, d0, halo)
            _, (b, m) = span(dy, h0, halo)
            return (pl.ds(a, n), pl.ds(b, m))
        return f

    vcopies = exchange(vol, rim_src(3, depth, height, 0), vt, rim_dst(3, depth, height), vsend, vrecv)
    ccopies = exchange(cot, rim_src(1, depth, height, 0), ct, rim_dst(1, depth, height), csend, crecv)

    rows = lax.broadcasted_iota(jnp.int32, (width, width), 0)
    lanes = lax.broadcasted_iota(jnp.int32, (width, width), 1)
    for n, ref in enumerate((vol, cot)):
        total = jnp.zeros((depth * chans, width), F32)
        for y in range(height):
            pick = ((lanes == 8 * y + rows) & (rows < 8)) | ((lanes == 8 * y + rows - 56) & (rows >= 120))
            total = total + dot(ref[:, y].reshape(depth * chans, width), pick.astype(BF))
        pk[:, n] = total.astype(BF).reshape(depth, chans, width)
    zcopies = []
    for d, s in enumerate(zsteps):
        side = 0 if s > 0 else 1
        zcopies.append(pltpu.make_async_remote_copy(
            src_ref=pk, dst_ref=lr.at[1, pl.ds(3, depth), side],
            send_sem=zsend.at[d], recv_sem=zrecv.at[d],
            device_id=at(0, 0, s), device_id_type=MESH))
    begin(zcopies, zsends)
    begin(vcopies, sends)
    begin(ccopies, sends)
    vt[pl.ds(3, depth), pl.ds(3, height)] = vol[...]
    ct[pl.ds(1, depth), pl.ds(1, height)] = cot[...]
    landed(zcopies, zrecvs)

    def lr_src(dx, dy):
        (a, n), _ = span(dx, depth, 3)
        return (1, pl.ds(a + 3, n))

    def lr_dst(dx, dy):
        _, (a, n) = span(dx, depth, 3)
        return (1 - dy, pl.ds(a, n))

    lcopies = exchange(lr, lr_src, lr, lr_dst, lsend, lrecv)
    begin(lcopies, sends)
    landed(vcopies, recvs)
    landed(ccopies, recvs)
    landed(lcopies, recvs)

    def unpacked(tiles, dyi, yy, first, count, which):
        lo = (rows == 8 * yy + lanes - 56) & (lanes >= 120)
        hi = (rows == 8 * yy + lanes) & (lanes < 8)
        got = dot(lr[dyi, pl.ds(first, count), 0, which].reshape(count * chans, width), lo.astype(BF))
        got = got + dot(lr[dyi, pl.ds(first, count), 1, which].reshape(count * chans, width), hi.astype(BF))
        return jnp.concatenate([tiles.reshape(count * chans, width).astype(F32), got], axis=1)

    def shifted(wide, c):
        if c == 1:
            return wide
        return pltpu.roll(wide, 1 if c == 0 else wide.shape[1] - 1, 1)

    def fill_vol(y, _):
        wide = unpacked(vt[:, y], (y + 5) // 8, lax.rem(y + 5, 8), 0, depth + 6, 0)
        for c in range(3):
            vs[:, y, c] = shifted(wide, c).astype(BF).reshape(depth + 6, chans, 2 * width)

    lax.fori_loop(0, height + 6, fill_vol, None)

    def fill_cot(y, _):
        wide = unpacked(ct[:, y], (y + 7) // 8, lax.rem(y + 7, 8), 2, depth + 2, 1)
        for c in range(3):
            cs[:, y, c] = shifted(wide, c).astype(BF).reshape(depth + 2, chans, 2 * width)

    lax.fori_loop(0, height + 2, fill_cot, None)

    fine = lax.broadcasted_iota(jnp.int32, (1, 2 * width), 1)
    coarse = lax.broadcasted_iota(jnp.int32, (1, width), 1)
    low_ok = jnp.where(iz > 0, 1.0, 0.0).astype(F32)
    high_ok = jnp.where(iz < nz - 1, 1.0, 0.0).astype(F32)
    fine_mask = jnp.where(fine < width, 1.0, jnp.where(fine < 3 * width // 2, high_ok, low_ok))
    coarse_mask = jnp.where(coarse < width // 2, 1.0, jnp.where(coarse < 3 * width // 4, high_ok, low_ok))
    own_coarse = coarse < width // 2

    def conv_row(weight, planes, outs):
        m = weight.shape[0] // 3
        ys = [dot(weight, x) for x in planes]
        return [ys[p][:m] + ys[p + 1][m:2 * m] + ys[p + 2][2 * m:] for p in range(outs)]

    def enc_row(q, _):
        k = 9 * chans
        pre = conv_row(we[...], [vs[p, pl.ds(q, 3)].reshape(k, 2 * width) for p in range(depth + 6)], depth + 4)
        gq = iy * height + q - 2
        yok = jnp.where((gq >= 0) & (gq < ny * height), 1.0, 0.0).astype(F32)
        for p in range(depth + 4):
            t = pre[p]
            sig = 1.0 / (1.0 + jnp.exp(-t))
            ok = yok
            if p < 2:
                ok = ok * jnp.where(ix > 0, 1.0, 0.0).astype(F32)
            if p >= depth + 2:
                ok = ok * jnp.where(ix < nx - 1, 1.0, 0.0).astype(F32)
            skip[p, q] = (t * sig * (fine_mask * ok)).astype(BF)
            if 2 <= p < depth + 2:
                slope[p - 2, q] = sig * (1.0 + t * (1.0 - sig)) * fine_mask

    lax.fori_loop(0, height + 4, enc_row, None)

    pool = (lax.broadcasted_iota(jnp.int32, (2 * width, width), 0) // 2
            == lax.broadcasted_iota(jnp.int32, (2 * width, width), 1)).astype(BF)

    def pool_row(q, _):
        rows_in = skip[:, pl.ds(2 * q, 2)].reshape((depth + 4) * 2 * chans, 2 * width)
        half = dot(rows_in, pool).reshape(cd + 2, 4, chans, width)
        mean = ((half[:, 0] + half[:, 1] + half[:, 2] + half[:, 3]) * 0.125).astype(BF)
        wide = mean.astype(F32).reshape((cd + 2) * chans, width)
        for c in range(3):
            ps[:, q, c] = shifted(wide, c).astype(BF).reshape(cd + 2, chans, width)

    lax.fori_loop(0, ch + 2, pool_row, None)

    def joined_row(q, _):
        k = 9 * chans
        sums = [jnp.zeros((chans, 2 * width), F32) for _ in range(cd)]
        for e in range(2):
            r = 2 * q + e
            out = conv_row(wdb[...], [cs[p, pl.ds(r, 3)].reshape(k, 2 * width) for p in range(depth + 2)], depth)
            for p in range(depth):
                jg[p, r] = out[p][:chans]
                sums[p // 2] = sums[p // 2] + out[p][chans:]
        for p in range(cd):
            hi = sums[p].astype(BF)
            ughi[p, q] = hi
            uglo[p, q] = (sums[p] - hi.astype(F32)).astype(BF)

    lax.fori_loop(0, ch, joined_row, None)
    flat = (cd * ch * chans, 2 * width)
    grad = dot(ughi[...].reshape(flat), pool) + dot(uglo[...].reshape(flat), pool)
    ug[...] = grad.astype(BF).reshape(ug.shape)

    for q in range(ch):
        k = 9 * chans
        pre = conv_row(wc[...], [ps[p, q:q + 3].reshape(k, width) for p in range(cd + 2)], cd)
        for p in range(cd):
            t = pre[p]
            sig = 1.0 / (1.0 + jnp.exp(-t))
            a = (t * sig * coarse_mask).astype(BF)
            act[p, q] = a
            uc[1 + p, 1 + q, 0:chans] = dot(upt[...], a).astype(BF)
            back = dot(up[...], ug[p, q])
            uc[1 + p, 1 + q, chans:3 * chans] = (back * (sig * (1.0 + t * (1.0 - sig)) * coarse_mask)).astype(BF)

    ucopies = exchange(uc, rim_src(1, cd, ch, 1), uc, rim_dst(1, cd, ch), usend, urecv)
    begin(ucopies, sends)

    group16 = lax.broadcasted_iota(jnp.int32, (1, width), 1) // 16
    group32 = lax.broadcasted_iota(jnp.int32, (1, width), 1) // 32

    def tap_sums(block, step, groups, gid):
        out = []
        for b in range(3):
            total = jnp.zeros((step, width), F32)
            for q in range(groups):
                total = jnp.where(gid == q, block[(q + b) * step:(q + b + 1) * step], total)
            size = width // 2
            while size >= width // groups:
                total = total + pltpu.roll(total, size, 1)
                size //= 2
            out.append(total)
        return out

    def put(first, value):
        gr[pl.ds(first // 8, value.shape[0] // 8)] = value.reshape(value.shape[0] // 8, 8, width)

    tail = jnp.zeros((3 * chans, width), F32)
    step = 3 * chans
    taps = []
    masked = [jnp.where(own_coarse, uc[1 + p, 1:1 + ch, chans:3 * chans].reshape(2 * chans * ch, width), 0)
              for p in range(cd)]
    for a in range(3):
        block = sum(dot_nt(ps[p + a].reshape((ch + 2) * step, width), masked[p]) for p in range(cd))
        taps += tap_sums(block, step, ch, group32)
    for half in range(2):
        total = jnp.zeros((step, width), F32)
        for g in range(4):
            total = jnp.where(group32 == g, taps[4 * half + g], total)
        put(144 + 48 * half, total)
    tail = jnp.where(group32 == 2, taps[8], tail)
    up_total = jnp.zeros((2 * chans, width), F32)
    for p in range(cd):
        for q in range(ch):
            g = jnp.where(own_coarse, ug[p, q], 0)
            up_total = up_total + dot_nt(act[p, q], jnp.concatenate([g] * 8, axis=0))
    up_total = jnp.concatenate([up_total, jnp.zeros((chans, width), F32)], axis=0)
    tail = jnp.where(group16 == 3, up_total, tail)

    def fill_skip(y, _):
        wide = skip[1:depth + 3, y + 1].reshape((depth + 2) * chans, 2 * width).astype(F32)
        for c in range(3):
            part = shifted(wide, c)[:, :width]
            js[:, y, c, 0:chans] = part.astype(BF).reshape(depth + 2, chans, width)

    lax.fori_loop(0, height + 2, fill_skip, None)
    landed(ucopies, recvs)

    def fill_coarse(y, _):
        wide = uc[:, y, chans:3 * chans].reshape((cd + 2) * 2 * chans, width).astype(F32)
        for c in range(3):
            gs[:, y, c] = shifted(wide, c).astype(BF).reshape(cd + 2, 2 * chans, width)

    lax.fori_loop(0, ch + 2, fill_coarse, None)
    spread = (lax.broadcasted_iota(jnp.int32, (width, 2 * width), 1) // 2
              == lax.broadcasted_iota(jnp.int32, (width, 2 * width), 0)).astype(BF)

    def back_row(q, _):
        k = 18 * chans
        pg = conv_row(wcb[...], [gs[p, pl.ds(q, 3)].reshape(k, width) for p in range(cd + 2)], cd)
        for p in range(cd):
            v = pg[p] * 0.125
            hi = v.astype(BF)
            lo = (v - hi.astype(F32)).astype(BF)
            wide = dot(hi, spread) + dot(lo, spread)
            for e in range(2):
                for f in range(2):
                    g = (jg[2 * p + e, 2 * q + f] + wide) * slope[2 * p + e, 2 * q + f + 2]
                    eh[1 + 2 * p + e, 1 + 2 * q + f] = g.astype(BF)

    lax.fori_loop(0, ch, back_row, None)
    ecopies = exchange(eh, rim_src(1, depth, height, 1), eh, rim_dst(1, depth, height), esend, erecv)
    begin(ecopies, sends)

    low = lax.broadcasted_iota(jnp.int32, (width, width), 0)
    lane = lax.broadcasted_iota(jnp.int32, (width, width), 1)
    for c in range(3):
        source = lax.rem(lane + (c - 1) + 2 * width, 2 * width) // 2
        pick = (low == source).astype(BF)
        wide = dot(uc[:, :, 0:chans].reshape((cd + 2) * (ch + 2) * chans, width), pick)
        wide = wide.astype(BF).reshape(cd + 2, ch + 2, chans, width)
        for x in range(depth + 2):
            for y in range(height + 2):
                js[x, y, c, chans:2 * chans] = wide[(x + 1) // 2, (y + 1) // 2]

    def fine_taps(source, step, grads):
        taps = []
        for a in range(3):
            block = sum(dot_nt(source(a + p), grads[p]) for p in range(depth))
            taps += tap_sums(block, step, height, group16)
        total = jnp.zeros((step, width), F32)
        for g in range(8):
            total = jnp.where(group16 == g, taps[g], total)
        return total, taps[8]

    total, last = fine_taps(
        lambda x: js[x].reshape((height + 2) * 6 * chans, width), 6 * chans,
        [cot[p].reshape(height * chans, width) for p in range(depth)])
    put(48, total)
    tail = jnp.where(group16 == 1, last[:48], tail)
    tail = jnp.where(group16 == 2, last[48:], tail)
    total, last = fine_taps(
        lambda x: vs[x + 2, 2:height + 4, :, :, 0:width].reshape((height + 2) * 3 * chans, width), 3 * chans,
        [eh[1 + p, 1:1 + height, :, 0:width].reshape(height * chans, width) for p in range(depth)])
    put(0, total)
    tail = jnp.where(group16 == 0, last, tail)
    put(240, tail)
    used = 288 // 8
    if gr.shape[0] > used:
        gr[used:] = jnp.zeros((gr.shape[0] - used, 8, width), F32)

    per = gr.shape[0] // nx

    def ring(phase, axis, count, src_of, dst):
        me = (ix, iy, iz)[axis]
        out, got = [], []
        for k in range(1, count):
            to = lax.rem(me + k, count)
            frm = lax.rem(me - k + count, count)
            there = tuple(to if i == axis else v for i, v in enumerate((ix, iy, iz)))

            def copy(src, slot, there=there, k=k):
                return pltpu.make_async_remote_copy(
                    src_ref=src, dst_ref=dst(slot), send_sem=asend.at[phase, k - 1],
                    recv_sem=arecv.at[phase, k - 1], device_id=there, device_id_type=MESH)

            out.append(copy(src_of(to), me))
            got.append(copy(src_of(to), frm))
        for c in out:
            c.start()
        return out, got

    def arrived(copies):
        for c in copies[1]:
            c.wait_recv()

    first = ring(0, 0, nx, lambda to: gr.at[pl.ds(to * per, per)], lambda slot: rx.at[slot])
    rx[ix] = gr[pl.ds(ix * per, per)]

    def dec_row(q, _):
        k = 18 * chans
        out = conv_row(wd[...], [js[p, pl.ds(q, 3)].reshape(k, width) for p in range(depth + 2)], depth)
        for p in range(depth):
            dec_out[p, q] = out[p].astype(BF)

    lax.fori_loop(0, height // 2, dec_row, None)

    def summed(ref, count):
        total = ref[0]
        for k in range(1, count):
            total = total + ref[k]
        return total

    arrived(first)
    ry[iy] = summed(rx, nx)
    second = ring(1, 1, ny, lambda to: ry.at[iy], lambda slot: ry.at[slot])
    lax.fori_loop(height // 2, height, dec_row, None)
    landed(ecopies, recvs)

    def fill_enc(y, _):
        wide = eh[:, y].reshape((depth + 2) * chans, 2 * width).astype(F32)
        for c in range(3):
            part = shifted(wide, c)[:, :width]
            es[:, y, c] = part.astype(BF).reshape(depth + 2, chans, width)

    lax.fori_loop(0, height + 2, fill_enc, None)

    def vol_row(q, _):
        k = 9 * chans
        out = conv_row(web[...], [es[p, pl.ds(q, 3)].reshape(k, width) for p in range(depth + 2)], depth)
        for p in range(depth):
            vg_out[p, q] = out[p].astype(BF)

    arrived(second)
    rz[iz] = summed(ry, ny)
    third = ring(2, 2, nz, lambda to: rz.at[iz], lambda slot: rz.at[slot])
    lax.fori_loop(0, height // 2, vol_row, None)
    arrived(third)
    ag[ix] = summed(rz, nz)
    fourth = ring(3, 0, nx, lambda to: ag.at[ix], lambda slot: ag.at[slot])
    lax.fori_loop(height // 2, height, vol_row, None)
    arrived(fourth)
    sum_out[...] = ag[...].reshape(sum_out.shape)

    left(zcopies, zsends)
    for copies in (vcopies, ccopies, lcopies, ucopies, ecopies):
        left(copies, sends)
    for copies in (first, second, third, fourth):
        for c in copies[0]:
            c.wait_send()


def stacked(weight):
    k = 9 * weight.shape[1]
    return jnp.swapaxes(weight.reshape(3, k, weight.shape[2]), 1, 2).reshape(3 * weight.shape[2], k)


def flipped(weight):
    return jnp.transpose(weight[::-1], (0, 2, 1))


def per_device(sizes, volume, enc_weight, coarse_weight, up_weight, dec_weight, cotangent):
    nx, ny, nz = sizes
    chans, d, h, w = volume.shape
    cd, ch = d // 2, h // 2
    per = -(-36 // nx)
    vol = jnp.transpose(volume, (1, 2, 0, 3))
    cot = jnp.transpose(cotangent, (1, 2, 0, 3))
    operands = (
        vol, cot, stacked(enc_weight), stacked(dec_weight), stacked(flipped(dec_weight)),
        stacked(coarse_weight), stacked(flipped(coarse_weight)), stacked(flipped(enc_weight)),
        up_weight.T, up_weight)
    c2 = 2 * chans
    scratch = [
        ((d + 6, h + 6, chans, w), BF),
        ((d + 2, h + 2, chans, w), BF),
        ((d, 2, chans, w), BF),
        ((3, d + 6, 2, 2, chans, w), BF),
        ((d + 6, h + 6, 3, chans, 2 * w), BF),
        ((d + 2, h + 2, 3, chans, 2 * w), BF),
        ((d + 4, h + 4, chans, 2 * w), BF),
        ((d, h + 4, chans, 2 * w), F32),
        ((d, h, chans, 2 * w), F32),
        ((cd, ch, chans, 2 * w), BF),
        ((cd, ch, chans, 2 * w), BF),
        ((cd, ch, chans, w), BF),
        ((cd + 2, ch + 2, 3, chans, w), BF),
        ((cd, ch, c2, w), BF),
        ((cd + 2, ch + 2, 3 * chans, w), BF),
        ((cd + 2, ch + 2, 3, c2, w), BF),
        ((d + 2, h + 2, 3, c2, w), BF),
        ((d + 2, h + 2, chans, 2 * w), BF),
        ((d + 2, h + 2, 3, chans, w), BF),
        ((nx * per, 8, w), F32),
        ((nx, per, 8, w), F32),
        ((ny, per, 8, w), F32),
        ((nz, per, 8, w), F32),
        ((nx, per, 8, w), F32),
    ]
    dma = pltpu.SemaphoreType.DMA
    widest = max(sizes) - 1
    sems = [dma((8,))] * 4 + [dma((2,))] * 2 + [dma((8,))] * 6 + [dma((4, max(widest, 1)))] * 2
    vmem = pl.BlockSpec(memory_space=pltpu.VMEM)
    dec, vg, total = pl.pallas_call(
        functools.partial(kernel, sizes),
        out_shape=(
            jax.ShapeDtypeStruct((d, h, chans, w), BF),
            jax.ShapeDtypeStruct((d, h, chans, w), BF),
            jax.ShapeDtypeStruct((nx * per, 8, w), F32)),
        in_specs=[vmem] * len(operands),
        out_specs=(vmem,) * 3,
        scratch_shapes=[pltpu.VMEM(s, t) for s, t in scratch] + sems,
        compiler_params=pltpu.CompilerParams(
            collective_id=0, has_side_effects=True, vmem_limit_bytes=48 * 1024 * 1024),
    )(*operands)
    g = total.reshape(nx * per * 8, w)
    tail = g[240:288]
    enc = jnp.transpose(g[0:48].reshape(48, 8, 16), (1, 0, 2)).reshape(24, 16, 16)
    enc = jnp.concatenate([enc, tail[:, 0:16].reshape(3, 16, 16)], axis=0)
    decg = jnp.transpose(g[48:144].reshape(96, 8, 16), (1, 0, 2)).reshape(24, 32, 16)
    decl = jnp.concatenate([tail[:, 16:32], tail[:, 32:48]], axis=0).reshape(3, 32, 16)
    decg = jnp.concatenate([decg, decl], axis=0)
    coarse = jnp.transpose(g[144:240].reshape(2, 48, 4, 32), (0, 2, 1, 3)).reshape(24, 16, 32)
    coarse = jnp.concatenate([coarse, tail[:, 64:96].reshape(3, 16, 32)], axis=0)
    upg = tail[0:32, 48:64]
    return (jnp.transpose(dec, (2, 0, 1, 3)), jnp.transpose(vg, (2, 0, 1, 3)), enc, coarse, upg, decg)


def solution(mesh):
    sizes = tuple(mesh.shape[a] for a in AXES)
    spec = P(None, "gx", "gy", "gz")
    return jax.shard_map(
        functools.partial(per_device, sizes),
        mesh=mesh,
        in_specs=(spec, P(), P(), P(), P(), spec),
        out_specs=(spec, spec, P(), P(), P(), P()),
        check_vma=False,
    )
```

time: 551 us -> 90.4 us (0.16)
  waiting for transfers between devices: 294 us -> 0 us
  starting transfers between devices: 119 us -> 0 us
  Pallas kernels: 0 us -> 78.2 us
  local copies, waits for them, and re-layouts: 74 us -> 9.93 us
  matrix products: 27.5 us -> 0 us
  other arithmetic: 17.2 us -> 0.83 us
  between operations: 16.6 us -> 0.84 us
    psum x1 -> x0, waiting for transfers between devices: 253 us -> none  [packed_total(): total = lax.psum(jnp.concatenate([a.ravel() for a in arrays]), axis)]
    ppermute x36 -> x0, starting transfers between devices: 119 us -> none  [the longest x18 87.7 us: extended(): lax.ppermute(lax.slice_in_dim(block, block.shape[dim] - width, None, axis...]
    pallas_call x0 -> x1, Pallas kernels: none -> 78.2 us  [per_device(): pl.pallas_call(functools.partial(kernel, sizes), out_shape=(jax.ShapeDtyp...]
    ppermute x36 -> x0, waiting for transfers between devices: 40.7 us -> none  [the longest x18 27.9 us: extended(): lax.ppermute(lax.slice_in_dim(block, 0, width, axis=dim), axis, backward)]
    dot_general x84 -> x0, matrix products: 27.5 us -> none  [the longest x54 15.8 us: convolve(): jnp.einsum('ko,kxyz->oxyz', kernel, stacked, preferred_element_type=jnp.f...]
    reshape x63 -> x13, local copies, waits for them, and re-layouts: 28.5 us -> 1.62 us  [the longest x6 0.82 us: stacked(): weight.reshape(3, k, weight.shape[2])]
    slice x77 -> x5, local copies, waits for them, and re-layouts: 20.9 us -> 0.26 us  [the longest x1 0.08 us: per_device(): tail[:, 16:32]]
    concatenate x17 -> x4, other arithmetic: 10.1 us -> 0.83 us  [the longest x1 0.7 us: per_device(): jnp.concatenate([coarse, tail[:, 64:96].reshape(3, 16, 32)], axis=0)]
  transfers between devices with their start and end apart: 37 -> 0, of which waited for: 11 -> 0; matrix products, arithmetic and copies ran while one was open for 18% -> 0% of each run, Pallas kernels for 0% -> 0%
where the time goes in v1:
time: 90.4 us; the launch traced here: 89.8 us
  Pallas kernels  78.2 us (87%)
  local copies, waits for them, and re-layouts  9.93 us (11%)
    pallas_call x1, Pallas kernels, per_device(): pl.pallas_call(functools.partial(kernel, sizes), out_shape=(jax.ShapeDtyp...  78.2 us
    unnamed x18, local copies, waits for them, and re-layouts  6.27 us

profile of v1, /device:TPU:1, one launch (start us, length us, event | category | flops | bytes accessed | tf_op | source)
XLA Modules:
  0.0 89.8 jit_solution(11256944205514459766)
XLA Ops:
  0.6 1.1 %copy_bitcast_fusion = (bf16[4,8,16,128]{3,2,1,0:T(8,128)(2,1)S(1)}, bf16[4,8,16,128]{3,2,1,0:T(8,128)(2,1)S(1)}) fusion(bf16[16,4,8,128]{3,2,1,0:T(8,128)(2,1)} %param.11, bf16[16,4,8,128]{3,2,1,0:T(8,128)(2,1)} %param.6), kind=kLoop, calls=%fused_computation.3 | loop fusion | bytes 524288 | tf_op jit(solution)/shard_map/transpose | solution.py:478
  1.8 0.1 reshape.91
  2.0 0.8 copy-done.3
  2.9 0.2 copy.54
  3.1 0.1 reshape.93
  3.3 0.7 copy-done.2
  4.0 0.1 reshape.85
  4.2 0.2 copy.46
  4.4 0.2 reshape.83
  4.6 0.1 copy.50
  4.7 0.1 copy.51
  4.8 0.6 copy-done
  5.5 78.2 %shard_map.109 = (bf16[4,8,16,128]{3,2,1,0:T(8,128)(2,1)S(1)}, bf16[4,8,16,128]{3,2,1,0:T(8,128)(2,1)S(1)}, f32[40,8,128]{2,1,0:T(8,128)S(1)}) custom-call(bf16[4,8,16,128]{3,2,1,0:T(8,128)(2,1)S(1)} %get-tuple-element.38.vol, bf16[4,8,16,128]{3,2,1,0:T(8,128)(2,1)S(1)} %get-tuple-element.37.cot, bf16[48,144]{1,0:T(8,128)(2,1)S(1)} %bitcast.57, ...), custom_call_target="tpu_custom_call" | custom-call | tf_op jit(solution)/shard_map/pallas_call | solution.py:514
  84.1 0.2 reshape.101
  84.3 0.2 copy.61
  84.4 0.1 reshape.102
  84.6 0.8 copy.67
  85.6 0.1 copy.57
  85.9 0.8 copy.66
  86.8 0.1 reshape.98
  87.0 0.7 pad_maximum_fusion.2
  87.7 0.7 copy.69
  88.4 0.7 copy.64
  89.1 0.7 copy.65
  (30 shorter events, 1.2 us)
Async XLA Ops:
  0.6 1.1 %copy-start.1 = (bf16[27,16,32]{2,1,0:T(8,128)(2,1)S(1)}, bf16[27,16,32]{2,1,0:T(8,128)(2,1)}, u32[]{:S(2)}) copy-start(bf16[27,16,32]{2,1,0:T(8,128)(2,1)} %param.8) | copy-start | bytes 82948
  2.0 0.8 copy-start.3
  3.1 0.9 %copy-start.2 = (bf16[27,32,16]{1,2,0:T(8,128)(2,1)S(1)}, bf16[27,32,16]{1,2,0:T(8,128)(2,1)}, u32[]{:S(2)}) copy-start(bf16[27,32,16]{1,2,0:T(8,128)(2,1)} %param.10) | copy-start | bytes 82948
  4.7 0.7 copy-start

commit v2 on v1

v2 whole, which is shorter than its diff:
```python
import functools

import jax
import jax.numpy as jnp
from jax import lax
from jax.experimental import pallas as pl
from jax.experimental.pallas import tpu as pltpu
from jax.sharding import PartitionSpec as P

AXES = ("gx", "gy", "gz")
BF = jnp.bfloat16
F32 = jnp.float32
MESH = pl.DeviceIdType.MESH
DIRS = tuple((dx, dy) for dx in (-1, 0, 1) for dy in (-1, 0, 1) if (dx, dy) != (0, 0))


def dot(a, b):
    return jnp.dot(a, b, preferred_element_type=F32)


def dot_nt(a, b):
    return lax.dot_general(a, b, (((1,), (1,)), ((), ())), preferred_element_type=F32)


def all_of(*conds):
    total = None
    for c in conds:
        if c is not None:
            total = c if total is None else jnp.logical_and(total, c)
    return total


def span(step, size, halo):
    if step == 0:
        return (0, size), (halo, size)
    if step > 0:
        return (size - halo, halo), (0, halo)
    return (0, halo), (halo + size, halo)


def kernel(sizes, vc, we, wd, wdb, wc, wcb, web, upt, up, dec_out, vg_out, sum_out,
           vct, pk, er, vs, cs, skip, slope, jg, ughi, uglo, ug, ph, ps, act, uh, gh, gs, js, eh, es,
           gr, ar,
           vsend, vrecv, zsend, zrecv, psend, precv, gsend, grecv, usend, urecv, ssend, srecv, esend, erecv,
           asend, arecv):
    nx, ny, nz = sizes
    ix, iy, iz = (lax.axis_index(a) for a in AXES)
    depth, height, _, width = vc.shape
    chans = vc.shape[2] // 2
    cd, ch = depth // 2, height // 2

    def exists(step, index, count):
        return None if step == 0 else (index + step < count if step > 0 else index + step >= 0)

    def at(dx, dy, dz=0):
        return (ix + dx, iy + dy, iz + dz)

    def guarded(cond, f):
        if cond is None:
            f()
        else:
            pl.when(cond)(f)

    sends = [all_of(exists(dx, ix, nx), exists(dy, iy, ny)) for dx, dy in DIRS]
    recvs = [all_of(exists(-dx, ix, nx), exists(-dy, iy, ny)) for dx, dy in DIRS]
    ends = tuple((dx, dy, s) for s in (-1, 1) for dx in (-1, 0, 1) for dy in (-1, 0, 1))
    esends = [all_of(exists(dx, ix, nx), exists(dy, iy, ny), exists(dz, iz, nz)) for dx, dy, dz in ends]
    erecvs = [all_of(exists(-dx, ix, nx), exists(-dy, iy, ny), exists(-dz, iz, nz)) for dx, dy, dz in ends]

    for ref in (vct, er, skip, ph, uh, gh, eh):
        ref[...] = jnp.zeros(ref.shape, ref.dtype)
    barrier = pltpu.get_barrier_semaphore()

    def greet(device):
        pl.semaphore_signal(barrier, inc=1, device_id=device, device_id_type=MESH)

    for k in range(1, nx):
        greet((lax.rem(ix + k, nx), iy, iz))
    for k in range(1, ny):
        greet((ix, lax.rem(iy + k, ny), iz))
    for k in range(1, nz):
        greet((ix, iy, lax.rem(iz + k, nz)))
    for dx, dy, dz in [d + (0,) for d in DIRS] + list(ends):
        if (dx != 0) + (dy != 0) + (dz != 0) > 1:
            guarded(all_of(exists(dx, ix, nx), exists(dy, iy, ny), exists(dz, iz, nz)),
                    lambda dx=dx, dy=dy, dz=dz: greet(at(dx, dy, dz)))

    def both(index, count):
        return (jnp.where(index > 0, 1, 0) + jnp.where(index < count - 1, 1, 0)).astype(jnp.int32)

    bx, by, bz = both(ix, nx), both(iy, ny), both(iz, nz)
    pl.semaphore_wait(barrier, nx + ny + nz - 3 + bx * by + bx * bz + by * bz + bx * by * bz)

    def exchange(src, src_at, dst, dst_at, send_sem, recv_sem):
        copies = []
        for d, (dx, dy) in enumerate(DIRS):
            copies.append(pltpu.make_async_remote_copy(
                src_ref=src.at[src_at(dx, dy)], dst_ref=dst.at[dst_at(dx, dy)],
                send_sem=send_sem.at[d], recv_sem=recv_sem.at[d],
                device_id=at(dx, dy), device_id_type=MESH))
        return copies

    def begin(copies, conds):
        for c, s in zip(copies, conds):
            guarded(s, c.start)

    def landed(copies, conds):
        for c, r in zip(copies, conds):
            guarded(r, c.wait_recv)

    def left(copies, conds):
        for c, s in zip(copies, conds):
            guarded(s, c.wait_send)

    def rim_src(halo, d0, h0, off):
        def f(dx, dy):
            (a, n), _ = span(dx, d0, halo)
            (b, m), _ = span(dy, h0, halo)
            return (pl.ds(a + off, n), pl.ds(b + off, m))
        return f

    def rim_dst(halo, d0, h0):
        def f(dx, dy):
            _, (a, n) = span(dx, d0, halo)
            _, (b, m) = span(dy, h0, halo)
            return (pl.ds(a, n), pl.ds(b, m))
        return f

    vcopies = exchange(vc, rim_src(1, depth, height, 0), vct, rim_dst(1, depth, height), vsend, vrecv)
    begin(vcopies, sends)

    row = lax.broadcasted_iota(jnp.int32, (width, 2 * width), 0)
    lane = lax.broadcasted_iota(jnp.int32, (width, 2 * width), 1)
    total = jnp.zeros((depth * chans, 2 * width), F32)
    for n in range(2):
        for y in range(height):
            base = 64 * n + 8 * y
            pick = ((lane == base + row) & (row < 8)) | ((lane == width + base + row - 120) & (row >= 120))
            total = total + dot(vc[:, y, n * chans:(n + 1) * chans].reshape(depth * chans, width), pick.astype(BF))
    for side in range(2):
        pk[side] = total[:, side * width:(side + 1) * width].astype(BF).reshape(depth, chans, width)
    zcopies = []
    for d, (dx, dy, dz) in enumerate(ends):
        (a, n), (b, m) = span(dx, depth, 1)
        side = 1 if dz > 0 else 0
        zcopies.append(pltpu.make_async_remote_copy(
            src_ref=pk.at[side, pl.ds(a, n)], dst_ref=er.at[side, 1 - dy, pl.ds(b, m)],
            send_sem=zsend.at[d], recv_sem=zrecv.at[d],
            device_id=at(dx, dy, dz), device_id_type=MESH))
    begin(zcopies, esends)
    vct[pl.ds(1, depth), pl.ds(1, height)] = vc[...]
    landed(vcopies, recvs)
    landed(zcopies, erecvs)

    def shifted(wide, c):
        if c == 1:
            return wide
        return pltpu.roll(wide, 1 if c == 0 else wide.shape[1] - 1, 1)

    def fill_inputs(y, _):
        dyi, base = (y + 7) // 8, 8 * lax.rem(y + 7, 8)
        flat = ((depth + 2) * chans, width)
        kind, spot = lane // width, lax.rem(lane, width)
        source = base + 64 * kind + spot
        lo = (row == source - 120) & (spot >= 120)
        hi = (row == source) & (spot < 8)
        got = dot(er[1, dyi].reshape(flat), lo.astype(BF)) + dot(er[0, dyi].reshape(flat), hi.astype(BF))
        for n, ref in enumerate((vs, cs)):
            own = vct[:, y, n * chans:(n + 1) * chans].reshape(flat).astype(F32)
            wide = jnp.concatenate([own, got[:, n * width:(n + 1) * width]], axis=1)
            for c in range(3):
                ref[:, y, c] = shifted(wide, c).astype(BF).reshape(depth + 2, chans, 2 * width)

    lax.fori_loop(0, height + 2, fill_inputs, None)

    fine = lax.broadcasted_iota(jnp.int32, (1, 2 * width), 1)
    coarse = lax.broadcasted_iota(jnp.int32, (1, width), 1)
    low_ok = jnp.where(iz > 0, 1.0, 0.0).astype(F32)
    high_ok = jnp.where(iz < nz - 1, 1.0, 0.0).astype(F32)
    fine_mask = jnp.where(fine < width, 1.0, jnp.where(fine < 3 * width // 2, high_ok, low_ok))
    coarse_mask = jnp.where(coarse < width // 2, 1.0, jnp.where(coarse < 3 * width // 4, high_ok, low_ok))
    own_coarse = coarse < width // 2

    def conv_row(weight, planes, outs):
        m = weight.shape[0] // 3
        ys = [dot(weight, x) for x in planes]
        return [ys[p][:m] + ys[p + 1][m:2 * m] + ys[p + 2][2 * m:] for p in range(outs)]

    def enc_row(q, _):
        k = 9 * chans
        pre = conv_row(we[...], [vs[p, pl.ds(q, 3)].reshape(k, 2 * width) for p in range(depth + 2)], depth)
        for p in range(depth):
            t = pre[p]
            sig = 1.0 / (1.0 + jnp.exp(-t))
            skip[1 + p, 1 + q] = (t * sig * fine_mask).astype(BF)
            slope[p, q] = sig * (1.0 + t * (1.0 - sig)) * fine_mask

    lax.fori_loop(0, height, enc_row, None)

    pool = (lax.broadcasted_iota(jnp.int32, (2 * width, width), 0) // 2
            == lax.broadcasted_iota(jnp.int32, (2 * width, width), 1)).astype(BF)

    for q in range(ch):
        rows_in = skip[1:1 + depth, 1 + 2 * q:3 + 2 * q].reshape(depth * 2 * chans, 2 * width)
        half = dot(rows_in, pool).reshape(cd, 4, chans, width)
        ph[1:1 + cd, 1 + q] = ((half[:, 0] + half[:, 1] + half[:, 2] + half[:, 3]) * 0.125).astype(BF)
    pcopies = exchange(ph, rim_src(1, cd, ch, 1), ph, rim_dst(1, cd, ch), psend, precv)
    begin(pcopies, sends)

    def joined_row(q, _):
        k = 9 * chans
        sums = [jnp.zeros((chans, 2 * width), F32) for _ in range(cd)]
        for e in range(2):
            r = 2 * q + e
            out = conv_row(wdb[...], [cs[p, pl.ds(r, 3)].reshape(k, 2 * width) for p in range(depth + 2)], depth)
            for p in range(depth):
                jg[p, r] = out[p][:chans]
                sums[p // 2] = sums[p // 2] + out[p][chans:]
        for p in range(cd):
            hi = sums[p].astype(BF)
            ughi[p, q] = hi
            uglo[p, q] = (sums[p] - hi.astype(F32)).astype(BF)

    lax.fori_loop(0, ch, joined_row, None)
    flat = (cd * ch * chans, 2 * width)
    grad = dot(ughi[...].reshape(flat), pool) + dot(uglo[...].reshape(flat), pool)
    ug[...] = grad.astype(BF).reshape(ug.shape)

    landed(pcopies, recvs)

    def fill_pooled(q, _):
        wide = ph[:, q].reshape((cd + 2) * chans, width).astype(F32)
        for c in range(3):
            ps[:, q, c] = shifted(wide, c).astype(BF).reshape(cd + 2, chans, width)

    lax.fori_loop(0, ch + 2, fill_pooled, None)
    for q in range(ch):
        k = 9 * chans
        pre = conv_row(wc[...], [ps[p, q:q + 3].reshape(k, width) for p in range(cd + 2)], cd)
        for p in range(cd):
            t = pre[p]
            sig = 1.0 / (1.0 + jnp.exp(-t))
            a = (t * sig * coarse_mask).astype(BF)
            act[p, q] = a
            uh[1 + p, 1 + q] = dot(upt[...], a).astype(BF)
            back = dot(up[...], ug[p, q])
            gh[1 + p, 1 + q] = (back * (sig * (1.0 + t * (1.0 - sig)) * coarse_mask)).astype(BF)

    gcopies = exchange(gh, rim_src(1, cd, ch, 1), gh, rim_dst(1, cd, ch), gsend, grecv)
    begin(gcopies, sends)
    ucopies = exchange(uh, rim_src(1, cd, ch, 1), uh, rim_dst(1, cd, ch), usend, urecv)
    begin(ucopies, sends)
    scopies = exchange(skip, rim_src(1, depth, height, 1), skip, rim_dst(1, depth, height), ssend, srecv)
    begin(scopies, sends)

    group16 = lax.broadcasted_iota(jnp.int32, (1, width), 1) // 16
    group32 = lax.broadcasted_iota(jnp.int32, (1, width), 1) // 32

    def tap_sums(block, step, groups, gid):
        out = []
        for b in range(3):
            total = jnp.zeros((step, width), F32)
            for q in range(groups):
                total = jnp.where(gid == q, block[(q + b) * step:(q + b + 1) * step], total)
            size = width // 2
            while size >= width // groups:
                total = total + pltpu.roll(total, size, 1)
                size //= 2
            out.append(total)
        return out

    def put(first, value):
        part, tile = first // 96, first % 96 // 16
        gr[part, tile:tile + 3] = value.astype(BF).reshape(3, 16, width)

    tail = jnp.zeros((3 * chans, width), F32)
    step = 3 * chans
    taps = []
    masked = [jnp.where(own_coarse, gh[1 + p, 1:1 + ch].reshape(2 * chans * ch, width), 0)
              for p in range(cd)]
    for a in range(3):
        block = sum(dot_nt(ps[p + a].reshape((ch + 2) * step, width), masked[p]) for p in range(cd))
        taps += tap_sums(block, step, ch, group32)
    for half in range(2):
        total = jnp.zeros((step, width), F32)
        for g in range(4):
            total = jnp.where(group32 == g, taps[4 * half + g], total)
        put(144 + 48 * half, total)
    tail = jnp.where(group32 == 2, taps[8], tail)
    up_total = jnp.zeros((2 * chans, width), F32)
    for p in range(cd):
        for q in range(ch):
            g = jnp.where(own_coarse, ug[p, q], 0)
            up_total = up_total + dot_nt(act[p, q], jnp.concatenate([g] * 8, axis=0))
    up_total = jnp.concatenate([up_total, jnp.zeros((chans, width), F32)], axis=0)
    tail = jnp.where(group16 == 3, up_total, tail)

    def fill_skip(first, count, y):
        wide = skip[first:first + count, y].reshape(count * chans, 2 * width).astype(F32)
        for c in range(3):
            part = shifted(wide, c)[:, :width]
            js[first:first + count, y, c, 0:chans] = part.astype(BF).reshape(count, chans, width)

    lax.fori_loop(1, height + 1, lambda y, _: fill_skip(1, depth, y), None)
    landed(gcopies, recvs)

    def fill_coarse(y, _):
        wide = gh[:, y].reshape((cd + 2) * 2 * chans, width).astype(F32)
        for c in range(3):
            gs[:, y, c] = shifted(wide, c).astype(BF).reshape(cd + 2, 2 * chans, width)

    lax.fori_loop(0, ch + 2, fill_coarse, None)
    spread = (lax.broadcasted_iota(jnp.int32, (width, 2 * width), 1) // 2
              == lax.broadcasted_iota(jnp.int32, (width, 2 * width), 0)).astype(BF)

    def back_row(q, _):
        k = 18 * chans
        pg = conv_row(wcb[...], [gs[p, pl.ds(q, 3)].reshape(k, width) for p in range(cd + 2)], cd)
        for p in range(cd):
            v = pg[p] * 0.125
            hi = v.astype(BF)
            lo = (v - hi.astype(F32)).astype(BF)
            wide = dot(hi, spread) + dot(lo, spread)
            for e in range(2):
                for f in range(2):
                    g = (jg[2 * p + e, 2 * q + f] + wide) * slope[2 * p + e, 2 * q + f]
                    eh[1 + 2 * p + e, 1 + 2 * q + f] = g.astype(BF)

    lax.fori_loop(0, ch, back_row, None)
    ecopies = exchange(eh, rim_src(1, depth, height, 1), eh, rim_dst(1, depth, height), esend, erecv)
    begin(ecopies, sends)

    landed(ucopies, recvs)
    low = lax.broadcasted_iota(jnp.int32, (width, width), 0)
    lane = lax.broadcasted_iota(jnp.int32, (width, width), 1)
    for c in range(3):
        source = lax.rem(lane + (c - 1) + 2 * width, 2 * width) // 2
        pick = (low == source).astype(BF)
        wide = dot(uh[...].reshape((cd + 2) * (ch + 2) * chans, width), pick)
        wide = wide.astype(BF).reshape(cd + 2, ch + 2, chans, width)
        for x in range(depth + 2):
            for y in range(height + 2):
                js[x, y, c, chans:2 * chans] = wide[(x + 1) // 2, (y + 1) // 2]
    landed(scopies, recvs)
    for y in (0, height + 1):
        fill_skip(0, depth + 2, y)

    def fill_sides(y, _):
        fill_skip(0, 1, y)
        fill_skip(depth + 1, 1, y)

    lax.fori_loop(1, height + 1, fill_sides, None)

    def fine_taps(source, step, grads):
        taps = []
        for a in range(3):
            block = sum(dot_nt(source(a + p), grads[p]) for p in range(depth))
            taps += tap_sums(block, step, height, group16)
        total = jnp.zeros((step, width), F32)
        for g in range(8):
            total = jnp.where(group16 == g, taps[g], total)
        return total, taps[8]

    total, last = fine_taps(
        lambda x: js[x].reshape((height + 2) * 6 * chans, width), 6 * chans,
        [vc[p, :, chans:2 * chans].reshape(height * chans, width) for p in range(depth)])
    put(48, total[:48])
    put(96, total[48:])
    tail = jnp.where(group16 == 1, last[:48], tail)
    tail = jnp.where(group16 == 2, last[48:], tail)
    total, last = fine_taps(
        lambda x: vs[x, :, :, :, 0:width].reshape((height + 2) * 3 * chans, width), 3 * chans,
        [eh[1 + p, 1:1 + height, :, 0:width].reshape(height * chans, width) for p in range(depth)])
    put(0, total)
    tail = jnp.where(group16 == 0, last, tail)
    put(240, tail)
    used = 96 // 16
    if gr.shape[1] > used:
        gr[:, used:] = jnp.zeros((3, gr.shape[1] - used, 16, width), BF)

    here = (ix, iy, iz)

    def ring(phase):
        out, got = [], []
        for part in range(3):
            axis = (part + phase % 3) % 3
            count, me = sizes[axis], here[axis]
            per = gr.shape[1] // sizes[part]
            for k in range(1, count):
                to = lax.rem(me + k, count)
                frm = lax.rem(me - k + count, count)
                there = tuple(to if i == axis else v for i, v in enumerate(here))
                src = gr.at[part, pl.ds(to * per, per)] if phase == 0 else ar.at[phase, part, me]

                def copy(slot):
                    return pltpu.make_async_remote_copy(
                        src_ref=src, dst_ref=ar.at[phase, part, slot], send_sem=asend.at[phase, part, k - 1],
                        recv_sem=arecv.at[phase, part, k - 1], device_id=there, device_id_type=MESH)

                out.append(copy(me))
                got.append(copy(frm))
        for c in out:
            c.start()
        return out, got

    def advance(copies, phase):
        for c in copies[1]:
            c.wait_recv()
        for part in range(3):
            total = ar[phase, part, 0].astype(F32)
            for k in range(1, sizes[(part + phase) % 3]):
                total = total + ar[phase, part, k].astype(F32)
            ar[phase + 1, part, here[(part + phase + 1) % 3]] = total.astype(BF)
        return ring(phase + 1)

    first = ring(0)
    for part in range(3):
        per = gr.shape[1] // sizes[part]
        ar[0, part, here[part]] = gr[part, pl.ds(here[part] * per, per)]

    def dec_row(q, _):
        k = 18 * chans
        out = conv_row(wd[...], [js[p, pl.ds(q, 3)].reshape(k, width) for p in range(depth + 2)], depth)
        for p in range(depth):
            dec_out[p, q] = out[p].astype(BF)

    lax.fori_loop(0, height // 2, dec_row, None)

    second = advance(first, 0)
    lax.fori_loop(height // 2, height, dec_row, None)
    landed(ecopies, recvs)

    def fill_enc(y, _):
        wide = eh[:, y].reshape((depth + 2) * chans, 2 * width).astype(F32)
        for c in range(3):
            part = shifted(wide, c)[:, :width]
            es[:, y, c] = part.astype(BF).reshape(depth + 2, chans, width)

    lax.fori_loop(0, height + 2, fill_enc, None)

    def vol_row(q, _):
        k = 9 * chans
        out = conv_row(web[...], [es[p, pl.ds(q, 3)].reshape(k, width) for p in range(depth + 2)], depth)
        for p in range(depth):
            vg_out[p, q] = out[p].astype(BF)

    third = advance(second, 1)
    lax.fori_loop(0, height // 2, vol_row, None)
    fourth = advance(third, 2)
    lax.fori_loop(height // 2, height, vol_row, None)
    for c in fourth[1]:
        c.wait_recv()
    for part in range(3):
        sum_out[part] = ar[3, part].astype(F32).reshape(sum_out.shape[1:])

    left(zcopies, esends)
    for copies in (vcopies, pcopies, gcopies, ucopies, scopies, ecopies):
        left(copies, sends)
    for copies in (first, second, third, fourth):
        for c in copies[0]:
            c.wait_send()


def stacked(weight):
    k = 9 * weight.shape[1]
    return jnp.swapaxes(weight.reshape(3, k, weight.shape[2]), 1, 2).reshape(3 * weight.shape[2], k)


def flipped(weight):
    return jnp.transpose(weight[::-1], (0, 2, 1))


def per_device(sizes, volume, enc_weight, coarse_weight, up_weight, dec_weight, cotangent):
    nx, ny, nz = sizes
    chans, d, h, w = volume.shape
    cd, ch = d // 2, h // 2
    tiles = max(-(-6 // n) * n for n in sizes)
    pair = jnp.transpose(jnp.concatenate([volume, cotangent], axis=0), (1, 2, 0, 3))
    operands = (
        pair, stacked(enc_weight), stacked(dec_weight), stacked(flipped(dec_weight)),
        stacked(coarse_weight), stacked(flipped(coarse_weight)), stacked(flipped(enc_weight)),
        up_weight.T, up_weight)
    c2 = 2 * chans
    scratch = [
        ((d + 2, h + 2, c2, w), BF),
        ((2, d, chans, w), BF),
        ((2, 3, d + 2, chans, w), BF),
        ((d + 2, h + 2, 3, chans, 2 * w), BF),
        ((d + 2, h + 2, 3, chans, 2 * w), BF),
        ((d + 2, h + 2, chans, 2 * w), BF),
        ((d, h, chans, 2 * w), F32),
        ((d, h, chans, 2 * w), F32),
        ((cd, ch, chans, 2 * w), BF),
        ((cd, ch, chans, 2 * w), BF),
        ((cd, ch, chans, w), BF),
        ((cd + 2, ch + 2, chans, w), BF),
        ((cd + 2, ch + 2, 3, chans, w), BF),
        ((cd, ch, c2, w), BF),
        ((cd + 2, ch + 2, chans, w), BF),
        ((cd + 2, ch + 2, c2, w), BF),
        ((cd + 2, ch + 2, 3, c2, w), BF),
        ((d + 2, h + 2, 3, c2, w), BF),
        ((d + 2, h + 2, chans, 2 * w), BF),
        ((d + 2, h + 2, 3, chans, w), BF),
        ((3, tiles, 16, w), BF),
        ((4, 3, max(sizes), tiles // max(sizes), 16, w), BF),
    ]
    dma = pltpu.SemaphoreType.DMA
    widest = max(sizes) - 1
    sems = [dma((8,))] * 2 + [dma((18,))] * 2 + [dma((8,))] * 10 + [dma((4, 3, max(widest, 1)))] * 2
    vmem = pl.BlockSpec(memory_space=pltpu.VMEM)
    dec, vg, total = pl.pallas_call(
        functools.partial(kernel, sizes),
        out_shape=(
            jax.ShapeDtypeStruct((d, h, chans, w), BF),
            jax.ShapeDtypeStruct((d, h, chans, w), BF),
            jax.ShapeDtypeStruct((3, tiles, 16, w), F32)),
        in_specs=[vmem] * len(operands),
        out_specs=(vmem,) * 3,
        scratch_shapes=[pltpu.VMEM(s, t) for s, t in scratch] + sems,
        compiler_params=pltpu.CompilerParams(
            collective_id=0, has_side_effects=True, vmem_limit_bytes=48 * 1024 * 1024),
    )(*operands)
    g = total[:, :6].reshape(288, w)
    tail = g[240:288]
    enc = jnp.transpose(g[0:48].reshape(48, 8, 16), (1, 0, 2)).reshape(24, 16, 16)
    enc = jnp.concatenate([enc, tail[:, 0:16].reshape(3, 16, 16)], axis=0)
    decg = jnp.transpose(g[48:144].reshape(96, 8, 16), (1, 0, 2)).reshape(24, 32, 16)
    decl = jnp.concatenate([tail[:, 16:32], tail[:, 32:48]], axis=0).reshape(3, 32, 16)
    decg = jnp.concatenate([decg, decl], axis=0)
    coarse = jnp.transpose(g[144:240].reshape(2, 48, 4, 32), (0, 2, 1, 3)).reshape(24, 16, 32)
    coarse = jnp.concatenate([coarse, tail[:, 64:96].reshape(3, 16, 32)], axis=0)
    upg = tail[0:32, 48:64]
    return (jnp.transpose(dec, (2, 0, 1, 3)), jnp.transpose(vg, (2, 0, 1, 3)), enc, coarse, upg, decg)


def solution(mesh):
    sizes = tuple(mesh.shape[a] for a in AXES)
    spec = P(None, "gx", "gy", "gz")
    return jax.shard_map(
        functools.partial(per_device, sizes),
        mesh=mesh,
        in_specs=(spec, P(), P(), P(), P(), spec),
        out_specs=(spec, spec, P(), P(), P(), P()),
        check_vma=False,
    )
```

time: 90.4 us -> 87 us (0.962)
  the two profiles are of different devices: /device:TPU:1 before, /device:TPU:8 now
where the time goes in v2:
time: 87 us; the launch traced here: 86.7 us
  Pallas kernels  74.4 us (86%)
  local copies, waits for them, and re-layouts  10.6 us (12%)
  between operations  0.88 us (1%)
    pallas_call x1, Pallas kernels, per_device(): pl.pallas_call(functools.partial(kernel, sizes), out_shape=(jax.ShapeDtyp...  74.4 us
    unnamed x25, local copies, waits for them, and re-layouts  8.46 us

profile of v2, /device:TPU:8, one launch (start us, length us, event | category | flops | bytes accessed | tf_op | source)
XLA Modules:
  0.0 86.7 jit_solution(14093196520404029793)
XLA Ops:
  0.6 1.0 %copy.48 = bf16[16,4,8,128]{3,0,2,1:T(8,128)(2,1)S(1)} copy(bf16[16,4,8,128]{3,2,1,0:T(8,128)(2,1)} %param.11) | data formatting | bytes 262144 | tf_op args[5]
  1.7 0.8 copy-done.3
  2.5 0.2 copy.49
  2.8 0.1 reshape.78
  2.9 0.7 copy-done.2
  3.7 0.1 reshape.80
  3.9 0.1 copy.53
  4.0 0.8 copy-done.1
  4.8 0.1 copy.54
  4.9 0.1 reshape.86
  5.2 0.2 copy.57
  5.4 0.1 reshape.88
  5.6 0.7 copy-done
  6.3 74.4 %shard_map.109 = (bf16[4,8,16,128]{3,2,1,0:T(8,128)(2,1)S(1)}, bf16[4,8,16,128]{3,2,1,0:T(8,128)(2,1)S(1)}, f32[3,8,16,128]{3,2,1,0:T(8,128)S(1)}) custom-call(bf16[4,8,32,128]{3,2,1,0:T(8,128)(2,1)S(1)} %maximum_bitcast_fusion.vc, bf16[48,144]{1,0:T(8,128)(2,1)S(1)} %bitcast.59, bf16[48,288]{1,0:T(8,128)(2,1)S(1)} %bitcast.55, ...), custom_call_target="tpu_custom_call" | custom-call | tf_op jit(solution)/shard_map/pallas_call | solution.py:512
  80.7 0.7 copy.70
  81.4 0.7 copy.71
  82.4 0.1 reshape.92
  82.6 0.8 copy.72
  83.6 0.1 reshape.94
  83.7 0.1 copy.64
  83.9 0.7 pad_maximum_fusion.2
  84.6 0.7 copy.77
  85.7 0.1 reshape.98
  85.9 0.8 copy.73
  (36 shorter events, 1.4 us)
Async XLA Ops:
  0.6 1.0 %copy-start.4 = (bf16[16,4,8,128]{3,2,1,0:T(8,128)(2,1)S(1)}, bf16[16,4,8,128]{3,2,1,0:T(8,128)(2,1)}, u32[]{:S(2)}) copy-start(bf16[16,4,8,128]{3,2,1,0:T(8,128)(2,1)} %param.6) | copy-start | bytes 393220
  1.7 0.8 copy-start.3
  2.7 0.9 %copy-start.2 = (bf16[27,32,16]{1,2,0:T(8,128)(2,1)S(1)}, bf16[27,32,16]{1,2,0:T(8,128)(2,1)}, u32[]{:S(2)}) copy-start(bf16[27,32,16]{1,2,0:T(8,128)(2,1)} %param.10) | copy-start | bytes 82948
  3.9 0.9 %copy-start.1 = (bf16[27,16,32]{2,1,0:T(8,128)(2,1)S(1)}, bf16[27,16,32]{2,1,0:T(8,128)(2,1)}, u32[]{:S(2)}) copy-start(bf16[27,16,32]{2,1,0:T(8,128)(2,1)} %param.8) | copy-start | bytes 82948
  5.5 0.7 copy-start

commit v3 on v2

--- a/solution.py
+++ b/solution.py
@@ -67,67 +67,36 @@
     esends = [all_of(exists(dx, ix, nx), exists(dy, iy, ny), exists(dz, iz, nz)) for dx, dy, dz in ends]
     erecvs = [all_of(exists(-dx, ix, nx), exists(-dy, iy, ny), exists(-dz, iz, nz)) for dx, dy, dz in ends]
 
+    cores = min(2, nx)
+    lows, across = nx // cores, ny // 2 if ny > 4 else ny
+    highs = ny // across
+    core, y_low, x_at, y_high = lax.rem(ix, cores), ix // cores, lax.rem(iy, across), iy // across
+    groups = (
+        (cores * across, core * across + x_at,
+         lambda j: (y_low * cores + j // across, y_high * across + lax.rem(j, across), iz)),
+        (highs * lows, y_high * lows + y_low,
+         lambda j: (lax.rem(j, lows) * cores + core, (j // lows) * across + x_at, iz)),
+        (nz, iz, lambda j: (ix, iy, j)),
+    )
+
     for ref in (vct, er, skip, ph, uh, gh, eh):
         ref[...] = jnp.zeros(ref.shape, ref.dtype)
+    vct[1:1 + depth, 1:1 + height] = vc[...]
     barrier = pltpu.get_barrier_semaphore()
 
     def greet(device):
         pl.semaphore_signal(barrier, inc=1, device_id=device, device_id_type=MESH)
 
-    for k in range(1, nx):
-        greet((lax.rem(ix + k, nx), iy, iz))
-    for k in range(1, ny):
-        greet((ix, lax.rem(iy + k, ny), iz))
-    for k in range(1, nz):
-        greet((ix, iy, lax.rem(iz + k, nz)))
+    for count, me, member in groups:
+        for k in range(1, count):
+            greet(member(lax.rem(me + k, count)))
     for dx, dy, dz in [d + (0,) for d in DIRS] + list(ends):
-        if (dx != 0) + (dy != 0) + (dz != 0) > 1:
+        if dx != 0 or dy != 0:
             guarded(all_of(exists(dx, ix, nx), exists(dy, iy, ny), exists(dz, iz, nz)),
                     lambda dx=dx, dy=dy, dz=dz: greet(at(dx, dy, dz)))
 
     def both(index, count):
         return (jnp.where(index > 0, 1, 0) + jnp.where(index < count - 1, 1, 0)).astype(jnp.int32)
-
-    bx, by, bz = both(ix, nx), both(iy, ny), both(iz, nz)
-    pl.semaphore_wait(barrier, nx + ny + nz - 3 + bx * by + bx * bz + by * bz + bx * by * bz)
-
-    def exchange(src, src_at, dst, dst_at, send_sem, recv_sem):
-        copies = []
-        for d, (dx, dy) in enumerate(DIRS):
-            copies.append(pltpu.make_async_remote_copy(
-                src_ref=src.at[src_at(dx, dy)], dst_ref=dst.at[dst_at(dx, dy)],
-                send_sem=send_sem.at[d], recv_sem=recv_sem.at[d],
-                device_id=at(dx, dy), device_id_type=MESH))
-        return copies
-
-    def begin(copies, conds):
-        for c, s in zip(copies, conds):
-            guarded(s, c.start)
-
-    def landed(copies, conds):
-        for c, r in zip(copies, conds):
-            guarded(r, c.wait_recv)
-
-    def left(copies, conds):
-        for c, s in zip(copies, conds):
-            guarded(s, c.wait_send)
-
-    def rim_src(halo, d0, h0, off):
-        def f(dx, dy):
-            (a, n), _ = span(dx, d0, halo)
-            (b, m), _ = span(dy, h0, halo)
-            return (pl.ds(a + off, n), pl.ds(b + off, m))
-        return f
-
-    def rim_dst(halo, d0, h0):
-        def f(dx, dy):
-            _, (a, n) = span(dx, d0, halo)
-            _, (b, m) = span(dy, h0, halo)
-            return (pl.ds(a, n), pl.ds(b, m))
-        return f
-
-    vcopies = exchange(vc, rim_src(1, depth, height, 0), vct, rim_dst(1, depth, height), vsend, vrecv)
-    begin(vcopies, sends)
 
     row = lax.broadcasted_iota(jnp.int32, (width, 2 * width), 0)
     lane = lax.broadcasted_iota(jnp.int32, (width, 2 * width), 1)
@@ -139,6 +108,48 @@
             total = total + dot(vc[:, y, n * chans:(n + 1) * chans].reshape(depth * chans, width), pick.astype(BF))
     for side in range(2):
         pk[side] = total[:, side * width:(side + 1) * width].astype(BF).reshape(depth, chans, width)
+    bx, by, bz = both(ix, nx), both(iy, ny), both(iz, nz)
+    near = bx + by + bx * by
+    pl.semaphore_wait(barrier, sum(count - 1 for count, _, _ in groups) + near + near * bz)
+
+    def exchange(src, src_at, dst, dst_at, send_sem, recv_sem):
+        copies = []
+        for d, (dx, dy) in enumerate(DIRS):
+            copies.append(pltpu.make_async_remote_copy(
+                src_ref=src.at[src_at(dx, dy)], dst_ref=dst.at[dst_at(dx, dy)],
+                send_sem=send_sem.at[d], recv_sem=recv_sem.at[d],
+                device_id=at(dx, dy), device_id_type=MESH))
+        return copies
+
+    def begin(copies, conds):
+        for c, s in zip(copies, conds):
+            guarded(s, c.start)
+
+    def landed(copies, conds):
+        for c, r in zip(copies, conds):
+            guarded(r, c.wait_recv)
+
+    def left(copies, conds):
+        for c, s in zip(copies, conds):
+            guarded(s, c.wait_send)
+
+    def rim_src(halo, d0, h0, off):
+        def f(dx, dy):
+            (a, n), _ = span(dx, d0, halo)
+            (b, m), _ = span(dy, h0, halo)
+            return (pl.ds(a + off, n), pl.ds(b + off, m))
+        return f
+
+    def rim_dst(halo, d0, h0):
+        def f(dx, dy):
+            _, (a, n) = span(dx, d0, halo)
+            _, (b, m) = span(dy, h0, halo)
+            return (pl.ds(a, n), pl.ds(b, m))
+        return f
+
+    vcopies = exchange(vc, rim_src(1, depth, height, 0), vct, rim_dst(1, depth, height), vsend, vrecv)
+    begin(vcopies, sends)
+
     zcopies = []
     for d, (dx, dy, dz) in enumerate(ends):
         (a, n), (b, m) = span(dx, depth, 1)
@@ -148,7 +159,6 @@
             send_sem=zsend.at[d], recv_sem=zrecv.at[d],
             device_id=at(dx, dy, dz), device_id_type=MESH))
     begin(zcopies, esends)
-    vct[pl.ds(1, depth), pl.ds(1, height)] = vc[...]
     landed(vcopies, recvs)
     landed(zcopies, erecvs)
 
@@ -206,6 +216,8 @@
         ph[1:1 + cd, 1 + q] = ((half[:, 0] + half[:, 1] + half[:, 2] + half[:, 3]) * 0.125).astype(BF)
     pcopies = exchange(ph, rim_src(1, cd, ch, 1), ph, rim_dst(1, cd, ch), psend, precv)
     begin(pcopies, sends)
+    scopies = exchange(skip, rim_src(1, depth, height, 1), skip, rim_dst(1, depth, height), ssend, srecv)
+    begin(scopies, sends)
 
     def joined_row(q, _):
         k = 9 * chans
@@ -250,8 +262,6 @@
     begin(gcopies, sends)
     ucopies = exchange(uh, rim_src(1, cd, ch, 1), uh, rim_dst(1, cd, ch), usend, urecv)
     begin(ucopies, sends)
-    scopies = exchange(skip, rim_src(1, depth, height, 1), skip, rim_dst(1, depth, height), ssend, srecv)
-    begin(scopies, sends)
 
     group16 = lax.broadcasted_iota(jnp.int32, (1, width), 1) // 16
     group32 = lax.broadcasted_iota(jnp.int32, (1, width), 1) // 32
@@ -270,8 +280,7 @@
         return out
 
     def put(first, value):
-        part, tile = first // 96, first % 96 // 16
-        gr[part, tile:tile + 3] = value.astype(BF).reshape(3, 16, width)
+        gr[first // 16:first // 16 + 3] = value.astype(BF).reshape(3, 16, width)
 
     tail = jnp.zeros((3 * chans, width), F32)
     step = 3 * chans
@@ -302,6 +311,34 @@
             js[first:first + count, y, c, 0:chans] = part.astype(BF).reshape(count, chans, width)
 
     lax.fori_loop(1, height + 1, lambda y, _: fill_skip(1, depth, y), None)
+    landed(scopies, recvs)
+    for y in (0, height + 1):
+        fill_skip(0, depth + 2, y)
+
+    def fill_sides(y, _):
+        fill_skip(0, 1, y)
+        fill_skip(depth + 1, 1, y)
+
+    lax.fori_loop(1, height + 1, fill_sides, None)
+
+    def fine_taps(source, step, grads):
+        taps = []
+        for a in range(3):
+            block = sum(dot_nt(source(a + p), grads[p]) for p in range(depth))
+            taps += tap_sums(block, step, height, group16)
+        total = jnp.zeros((step, width), F32)
+        for g in range(8):
+            total = jnp.where(group16 == g, taps[g], total)
+        return total, taps[8]
+
+    def joined_taps(first):
+        return fine_taps(
+            lambda x: js[x, :, :, first:first + chans].reshape((height + 2) * 3 * chans, width), 3 * chans,
+            [vc[p, :, chans:2 * chans].reshape(height * chans, width) for p in range(depth)])
+
+    total, last = joined_taps(0)
+    put(48, total)
+    tail = jnp.where(group16 == 1, last, tail)
     landed(gcopies, recvs)
 
     def fill_coarse(y, _):
@@ -341,64 +378,37 @@
         for x in range(depth + 2):
             for y in range(height + 2):
                 js[x, y, c, chans:2 * chans] = wide[(x + 1) // 2, (y + 1) // 2]
-    landed(scopies, recvs)
-    for y in (0, height + 1):
-        fill_skip(0, depth + 2, y)
-
-    def fill_sides(y, _):
-        fill_skip(0, 1, y)
-        fill_skip(depth + 1, 1, y)
-
-    lax.fori_loop(1, height + 1, fill_sides, None)
-
-    def fine_taps(source, step, grads):
-        taps = []
-        for a in range(3):
-            block = sum(dot_nt(source(a + p), grads[p]) for p in range(depth))
-            taps += tap_sums(block, step, height, group16)
-        total = jnp.zeros((step, width), F32)
-        for g in range(8):
-            total = jnp.where(group16 == g, taps[g], total)
-        return total, taps[8]
-
-    total, last = fine_taps(
-        lambda x: js[x].reshape((height + 2) * 6 * chans, width), 6 * chans,
-        [vc[p, :, chans:2 * chans].reshape(height * chans, width) for p in range(depth)])
-    put(48, total[:48])
-    put(96, total[48:])
-    tail = jnp.where(group16 == 1, last[:48], tail)
-    tail = jnp.where(group16 == 2, last[48:], tail)
+
+    total, last = joined_taps(chans)
+    put(96, total)
+    tail = jnp.where(group16 == 2, last, tail)
     total, last = fine_taps(
         lambda x: vs[x, :, :, :, 0:width].reshape((height + 2) * 3 * chans, width), 3 * chans,
         [eh[1 + p, 1:1 + height, :, 0:width].reshape(height * chans, width) for p in range(depth)])
     put(0, total)
     tail = jnp.where(group16 == 0, last, tail)
     put(240, tail)
-    used = 96 // 16
-    if gr.shape[1] > used:
-        gr[:, used:] = jnp.zeros((3, gr.shape[1] - used, 16, width), BF)
-
-    here = (ix, iy, iz)
+    used = 288 // 16
+    if gr.shape[0] > used:
+        gr[used:] = jnp.zeros((gr.shape[0] - used, 16, width), BF)
+
+    per = gr.shape[0] // groups[0][0]
 
     def ring(phase):
+        count, me, member = groups[phase % 3]
         out, got = [], []
-        for part in range(3):
-            axis = (part + phase % 3) % 3
-            count, me = sizes[axis], here[axis]
-            per = gr.shape[1] // sizes[part]
-            for k in range(1, count):
-                to = lax.rem(me + k, count)
-                frm = lax.rem(me - k + count, count)
-                there = tuple(to if i == axis else v for i, v in enumerate(here))
-                src = gr.at[part, pl.ds(to * per, per)] if phase == 0 else ar.at[phase, part, me]
-
-                def copy(slot):
-                    return pltpu.make_async_remote_copy(
-                        src_ref=src, dst_ref=ar.at[phase, part, slot], send_sem=asend.at[phase, part, k - 1],
-                        recv_sem=arecv.at[phase, part, k - 1], device_id=there, device_id_type=MESH)
-
-                out.append(copy(me))
-                got.append(copy(frm))
+        for k in range(1, count):
+            to = lax.rem(me + k, count)
+            frm = lax.rem(me - k + count, count)
+            src = gr.at[pl.ds(to * per, per)] if phase == 0 else ar.at[phase, me]
+
+            def copy(slot):
+                return pltpu.make_async_remote_copy(
+                    src_ref=src, dst_ref=ar.at[phase, slot], send_sem=asend.at[phase, k - 1],
+                    recv_sem=arecv.at[phase, k - 1], device_id=member(to), device_id_type=MESH)
+
+            out.append(copy(me))
+            got.append(copy(frm))
         for c in out:
             c.start()
         return out, got
@@ -406,17 +416,14 @@
     def advance(copies, phase):
         for c in copies[1]:
             c.wait_recv()
-        for part in range(3):
-            total = ar[phase, part, 0].astype(F32)
-            for k in range(1, sizes[(part + phase) % 3]):
-                total = total + ar[phase, part, k].astype(F32)
-            ar[phase + 1, part, here[(part + phase + 1) % 3]] = total.astype(BF)
+        total = ar[phase, 0].astype(F32)
+        for k in range(1, groups[phase][0]):
+            total = total + ar[phase, k].astype(F32)
+        ar[phase + 1, groups[(phase + 1) % 3][1]] = total.astype(BF)
         return ring(phase + 1)
 
     first = ring(0)
-    for part in range(3):
-        per = gr.shape[1] // sizes[part]
-        ar[0, part, here[part]] = gr[part, pl.ds(here[part] * per, per)]
+    ar[0, groups[0][1]] = gr[pl.ds(groups[0][1] * per, per)]
 
     def dec_row(q, _):
         k = 18 * chans
@@ -450,8 +457,7 @@
     lax.fori_loop(height // 2, height, vol_row, None)
     for c in fourth[1]:
         c.wait_recv()
-    for part in range(3):
-        sum_out[part] = ar[3, part].astype(F32).reshape(sum_out.shape[1:])
+    sum_out[...] = ar[3, 0:groups[0][0]].astype(F32).reshape(sum_out.shape)
 
     left(zcopies, esends)
     for copies in (vcopies, pcopies, gcopies, ucopies, scopies, ecopies):
@@ -474,13 +480,15 @@
     nx, ny, nz = sizes
     chans, d, h, w = volume.shape
     cd, ch = d // 2, h // 2
-    tiles = max(-(-6 // n) * n for n in sizes)
+    owners = min(2, nx) * (ny // 2 if ny > 4 else ny)
+    per = -(-18 // owners)
     pair = jnp.transpose(jnp.concatenate([volume, cotangent], axis=0), (1, 2, 0, 3))
     operands = (
         pair, stacked(enc_weight), stacked(dec_weight), stacked(flipped(dec_weight)),
         stacked(coarse_weight), stacked(flipped(coarse_weight)), stacked(flipped(enc_weight)),
         up_weight.T, up_weight)
     c2 = 2 * chans
+    widest = max(owners, nx * ny // owners, nz) - 1
     scratch = [
         ((d + 2, h + 2, c2, w), BF),
         ((2, d, chans, w), BF),
@@ -502,32 +510,33 @@
         ((d + 2, h + 2, 3, c2, w), BF),
         ((d + 2, h + 2, chans, 2 * w), BF),
         ((d + 2, h + 2, 3, chans, w), BF),
-        ((3, tiles, 16, w), BF),
-        ((4, 3, max(sizes), tiles // max(sizes), 16, w), BF),
+        ((owners * per, 16, w), BF),
+        ((4, widest + 1, per, 16, w), BF),
     ]
     dma = pltpu.SemaphoreType.DMA
-    widest = max(sizes) - 1
-    sems = [dma((8,))] * 2 + [dma((18,))] * 2 + [dma((8,))] * 10 + [dma((4, 3, max(widest, 1)))] * 2
+    sems = [dma((8,))] * 2 + [dma((18,))] * 2 + [dma((8,))] * 10 + [dma((4, max(widest, 1)))] * 2
     vmem = pl.BlockSpec(memory_space=pltpu.VMEM)
     dec, vg, total = pl.pallas_call(
         functools.partial(kernel, sizes),
         out_shape=(
             jax.ShapeDtypeStruct((d, h, chans, w), BF),
             jax.ShapeDtypeStruct((d, h, chans, w), BF),
-            jax.ShapeDtypeStruct((3, tiles, 16, w), F32)),
+            jax.ShapeDtypeStruct((owners * per, 16, w), F32)),
         in_specs=[vmem] * len(operands),
         out_specs=(vmem,) * 3,
         scratch_shapes=[pltpu.VMEM(s, t) for s, t in scratch] + sems,
         compiler_params=pltpu.CompilerParams(
             collective_id=0, has_side_effects=True, vmem_limit_bytes=48 * 1024 * 1024),
     )(*operands)
-    g = total[:, :6].reshape(288, w)
+    g = total[:18].reshape(288, w)
     tail = g[240:288]
     enc = jnp.transpose(g[0:48].reshape(48, 8, 16), (1, 0, 2)).reshape(24, 16, 16)
     enc = jnp.concatenate([enc, tail[:, 0:16].reshape(3, 16, 16)], axis=0)
-    decg = jnp.transpose(g[48:144].reshape(96, 8, 16), (1, 0, 2)).reshape(24, 32, 16)
-    decl = jnp.concatenate([tail[:, 16:32], tail[:, 32:48]], axis=0).reshape(3, 32, 16)
-    decg = jnp.concatenate([decg, decl], axis=0)
+    halves = []
+    for first, lane in ((48, 16), (96, 32)):
+        half = jnp.transpose(g[first:first + 48].reshape(48, 8, 16), (1, 0, 2)).reshape(24, 16, 16)
+        halves.append(jnp.concatenate([half, tail[:, lane:lane + 16].reshape(3, 16, 16)], axis=0))
+    decg = jnp.concatenate(halves, axis=1)
     coarse = jnp.transpose(g[144:240].reshape(2, 48, 4, 32), (0, 2, 1, 3)).reshape(24, 16, 32)
     coarse = jnp.concatenate([coarse, tail[:, 64:96].reshape(3, 16, 32)], axis=0)
     upg = tail[0:32, 48:64]

time: 87 us -> 81 us (0.931)
  the two profiles are of different devices: /device:TPU:8 before, /device:TPU:1 now
where the time goes in v3:
time: 81 us; the launch traced here: 80.7 us
  Pallas kernels  68.1 us (84%)
  local copies, waits for them, and re-layouts  10.9 us (13%)
  other arithmetic  0.88 us (1%)
  between operations  0.87 us (1%)
    pallas_call x1, Pallas kernels, per_device(): pl.pallas_call(functools.partial(kernel, sizes), out_shape=(jax.ShapeDtyp...  68.1 us
    unnamed x20, local copies, waits for them, and re-layouts  8.05 us

profile of v3, /device:TPU:1, one launch (start us, length us, event | category | flops | bytes accessed | tf_op | source)
XLA Modules:
  0.0 80.7 jit_solution(12081673491838178365)
XLA Ops:
  0.6 1.0 %copy.45 = bf16[16,4,8,128]{3,0,2,1:T(8,128)(2,1)S(1)} copy(bf16[16,4,8,128]{3,2,1,0:T(8,128)(2,1)} %param.6) | data formatting | bytes 262144 | tf_op args[0]
  1.7 0.9 %copy-done.1 = bf16[27,16,32]{2,1,0:T(8,128)(2,1)S(1)} copy-done((bf16[27,16,32]{2,1,0:T(8,128)(2,1)S(1)}, bf16[27,16,32]{2,1,0:T(8,128)(2,1)}, u32[]{:S(2)}) %copy-start.1) | copy-done | bytes 27672
  2.7 0.1 reshape.102
  2.8 0.8 %copy-done.3 = bf16[27,16,16]{0,2,1:T(8,128)(2,1)S(1)} copy-done((bf16[27,16,16]{0,2,1:T(8,128)(2,1)S(1)}, bf16[27,16,16]{0,2,1:T(8,128)(2,1)}, u32[]{:S(2)}) %copy-start.3) | copy-done | bytes 13848
  3.7 0.2 copy.55
  3.9 0.1 reshape.104
  4.1 0.7 copy-done.2
  4.9 0.1 reshape.96
  5.0 0.2 copy.47
  5.2 0.2 reshape.94
  5.4 0.1 copy.51
  5.6 0.1 copy.52
  5.7 0.6 copy-done
  6.3 68.1 %shard_map.109 = (bf16[4,8,16,128]{3,2,1,0:T(8,128)(2,1)S(1)}, bf16[4,8,16,128]{3,2,1,0:T(8,128)(2,1)S(1)}, f32[24,16,128]{2,1,0:T(8,128)S(1)}) custom-call(bf16[4,8,32,128]{3,2,1,0:T(8,128)(2,1)S(1)} %maximum_bitcast_fusion.vc, bf16[48,144]{1,0:T(8,128)(2,1)S(1)} %bitcast.57, bf16[48,288]{1,0:T(8,128)(2,1)S(1)} %bitcast.53, bf16[96,144]{1,0:T(8,128)(2,1)S(1)} %bitcast.50, ...), custom_call_target="tpu_custom_call" | custom-call | tf_op jit(solution)/shard_map/pallas_call | solution.py:519
  74.7 0.1 reshape.112
  74.8 0.1 copy.62
  75.4 0.1 maximum_maximum_fusion
  75.5 0.8 %copy.69 = f32[27,32,16]{1,2,0:T(8,128)} copy(f32[27,32,16]{1,0,2:T(8,128)S(1)} %maximum_maximum_fusion) | data formatting | bytes 110592
  76.8 0.8 %copy.68 = f32[27,16,16]{0,2,1:T(8,128)} copy(f32[27,16,16]{1,0,2:T(8,128)S(1)} %pad_maximum_fusion) | data formatting | bytes 55296
  77.7 0.1 reshape.109
  77.9 0.7 pad_maximum_fusion.1
  78.7 0.7 copy.71
  79.3 0.7 copy.66
  80.0 0.7 copy.67
  (35 shorter events, 1.7 us)
Async XLA Ops:
  0.6 1.0 %copy-start.4 = (bf16[16,4,8,128]{3,2,1,0:T(8,128)(2,1)S(1)}, bf16[16,4,8,128]{3,2,1,0:T(8,128)(2,1)}, u32[]{:S(2)}) copy-start(bf16[16,4,8,128]{3,2,1,0:T(8,128)(2,1)} %param.11) | copy-start | bytes 393220
  1.7 0.9 %copy-start.1 = (bf16[27,16,32]{2,1,0:T(8,128)(2,1)S(1)}, bf16[27,16,32]{2,1,0:T(8,128)(2,1)}, u32[]{:S(2)}) copy-start(bf16[27,16,32]{2,1,0:T(8,128)(2,1)} %param.8) | copy-start | bytes 82948
  2.8 0.8 %copy-start.3 = (bf16[27,16,16]{0,2,1:T(8,128)(2,1)S(1)}, bf16[27,16,16]{0,2,1:T(8,128)(2,1)}, u32[]{:S(2)}) copy-start(bf16[27,16,16]{0,2,1:T(8,128)(2,1)} %param.7) | copy-start | bytes 41476
  3.9 0.9 %copy-start.2 = (bf16[27,32,16]{1,2,0:T(8,128)(2,1)S(1)}, bf16[27,32,16]{1,2,0:T(8,128)(2,1)}, u32[]{:S(2)}) copy-start(bf16[27,32,16]{1,2,0:T(8,128)(2,1)} %param.10) | copy-start | bytes 82948
  5.6 0.7 copy-start

commit v4 on v3

--- a/solution.py
+++ b/solution.py
@@ -22,6 +22,85 @@
     return lax.dot_general(a, b, (((1,), (1,)), ((), ())), preferred_element_type=F32)
 
 
+def dot_tn(a, b):
+    return lax.dot_general(a, b, (((0,), (0,)), ((), ())), preferred_element_type=F32)
+
+
+def zero_one(shape, rule):
+    return rule(lax.broadcasted_iota(jnp.int32, shape, 0), lax.broadcasted_iota(jnp.int32, shape, 1))
+
+
+def arrange_weights(enc, coarse, upt, dec, we, wd, wdb, wc, wcb, web, up):
+    flat = enc[...].reshape(256, 27)
+    same_in = zero_one((256, 144), lambda r, l: r // 16 == l % 16)
+    same_out = zero_one((256, 144), lambda r, l: r % 16 == l % 16)
+    fold_in = zero_one((16, 256), lambda r, l: r == l % 16).astype(BF)
+    fold_out = zero_one((16, 256), lambda r, l: r == l // 16).astype(BF)
+    for a in range(3):
+        ahead = dot(flat, zero_one((27, 144), lambda r, l: r == 9 * a + l // 16).astype(BF))
+        we[16 * a:16 * a + 16] = dot(fold_in, jnp.where(same_in, ahead, 0.0).astype(BF)).astype(BF)
+        back = dot(flat, zero_one((27, 144), lambda r, l: r == 26 - 9 * a - l // 16).astype(BF))
+        web[16 * a:16 * a + 16] = dot(fold_out, jnp.where(same_out, back, 0.0).astype(BF)).astype(BF)
+    totals = [0.0] * 4
+    for t in range(9):
+        wide = zero_one((32, 288), lambda r, l: l == 32 * t + r).astype(BF)
+        slim = zero_one((16, 144), lambda r, l: l == 16 * t + r).astype(BF)
+        ahead, back = (t, 9 + t, 18 + t), (26 - t, 17 - t, 8 - t)
+        totals[0] += dot(jnp.concatenate([dec[k] for k in ahead], axis=0), wide)
+        totals[1] += dot_tn(jnp.concatenate([dec[k] for k in back], axis=1), slim)
+        totals[2] += dot_tn(jnp.concatenate([coarse[k] for k in ahead], axis=1), slim)
+        totals[3] += dot(jnp.concatenate([coarse[k] for k in back], axis=0), wide)
+    for ref, total in zip((wd, wdb, wc, wcb), totals):
+        ref[...] = total.astype(BF)
+    up[...] = dot_tn(upt[...], zero_one((16, 16), lambda r, l: r == l).astype(BF)).astype(BF)
+
+
+def finish(dec, vg, total, dec_out, vg_out, enc_out, coarse_out, up_out, decg_out,
+           enc, coarse, up, decg, sems):
+    copies = [pltpu.make_async_copy(a, b, sems.at[k]) for k, (a, b) in enumerate(
+        ((dec, dec_out), (vg, vg_out), (enc, enc_out), (coarse, coarse_out), (up, up_out), (decg, decg_out)))]
+    copies[0].start()
+    copies[1].start()
+
+    def rows(first, count):
+        return total[first // 16:(first + count) // 16].reshape(count, 128)
+
+    eye = zero_one((128, 128), lambda r, l: r == l).astype(BF)
+    for c in range(3):
+        last = rows(240 + 16 * c, 16)
+        block = jnp.concatenate([rows(48 + 16 * c, 16), rows(96 + 16 * c, 16)], axis=0)
+        turned = dot_nt(eye, block).reshape(8, 16, 32)
+        for g in range(8):
+            decg[3 * g + c] = turned[g]
+        skip_last = dot_nt(zero_one((16, 128), lambda r, l: l == 16 + r).astype(BF), last)
+        upper_last = dot_nt(zero_one((16, 128), lambda r, l: l == 32 + r).astype(BF), last)
+        decg[24 + c] = jnp.concatenate([skip_last, upper_last], axis=1)
+    copies[5].start()
+    for c in range(3):
+        for half in range(2):
+            block = rows(144 + 48 * half + 16 * c, 16)
+            for g in range(4):
+                pick = zero_one((128, 32), lambda r, l: r == 32 * g + l).astype(BF)
+                coarse[3 * (4 * half + g) + c] = dot(block, pick)
+        pick = zero_one((128, 32), lambda r, l: r == 64 + l).astype(BF)
+        coarse[24 + c] = dot(rows(240 + 16 * c, 16), pick)
+    copies[3].start()
+    up[...] = dot_nt(zero_one((16, 128), lambda r, l: l == 48 + r).astype(BF), rows(240, 32))
+    copies[4].start()
+    grow = zero_one((256, 16), lambda r, l: l == r // 16).astype(BF)
+    same = zero_one((256, 128), lambda r, l: r % 16 == l % 16)
+    flat = jnp.zeros((256, 27), F32)
+    for c in range(3):
+        wide = jnp.where(same, dot(grow, rows(16 * c, 16)), 0.0).astype(BF)
+        flat = flat + dot(wide, zero_one((128, 27), lambda r, l: l == 3 * (r // 16) + c).astype(BF))
+        wide = jnp.where(same, dot(grow, rows(240 + 16 * c, 16)), 0.0).astype(BF)
+        flat = flat + dot(wide, zero_one((128, 27), lambda r, l: (r < 16) & (l == 24 + c)).astype(BF))
+    enc[...] = flat.reshape(16, 16, 27)
+    copies[2].start()
+    for c in copies:
+        c.wait()
+
+
 def all_of(*conds):
     total = None
     for c in conds:
@@ -38,11 +117,12 @@
     return (0, halo), (halo + size, halo)
 
 
-def kernel(sizes, vc, we, wd, wdb, wc, wcb, web, upt, up, dec_out, vg_out, sum_out,
+def kernel(sizes, vc, enc_in, coarse_in, upt_in, dec_in, dec_out, vg_out, sum_out,
+           enc_w, coarse_w, upt, dec_w, we, wd, wdb, wc, wcb, web, up, turn,
            vct, pk, er, vs, cs, skip, slope, jg, ughi, uglo, ug, ph, ps, act, uh, gh, gs, js, eh, es,
            gr, ar,
            vsend, vrecv, zsend, zrecv, psend, precv, gsend, grecv, usend, urecv, ssend, srecv, esend, erecv,
-           asend, arecv):
+           asend, arecv, wsem):
     nx, ny, nz = sizes
     ix, iy, iz = (lax.axis_index(a) for a in AXES)
     depth, height, _, width = vc.shape
@@ -78,6 +158,11 @@
          lambda j: (lax.rem(j, lows) * cores + core, (j // lows) * across + x_at, iz)),
         (nz, iz, lambda j: (ix, iy, j)),
     )
+
+    loads = [pltpu.make_async_copy(a, b, wsem.at[k]) for k, (a, b) in enumerate(
+        ((enc_in, enc_w), (coarse_in, coarse_w), (upt_in, upt), (dec_in, dec_w)))]
+    for c in loads:
+        c.start()
 
     for ref in (vct, er, skip, ph, uh, gh, eh):
         ref[...] = jnp.zeros(ref.shape, ref.dtype)
@@ -159,6 +244,9 @@
             send_sem=zsend.at[d], recv_sem=zrecv.at[d],
             device_id=at(dx, dy, dz), device_id_type=MESH))
     begin(zcopies, esends)
+    for c in loads:
+        c.wait()
+    arrange_weights(enc_w, coarse_w, upt, dec_w, we, wd, wdb, wc, wcb, web, up)
     landed(vcopies, recvs)
     landed(zcopies, erecvs)
 
@@ -425,16 +513,25 @@
     first = ring(0)
     ar[0, groups[0][1]] = gr[pl.ds(groups[0][1] * per, per)]
 
+    order = zero_one((height * chans, height * chans),
+                     lambda r, l: (r // height == l % chans) & (r % height == l // chans)).astype(BF)
+
+    def channels_first(which, ref):
+        for p in range(depth):
+            moved = dot(order, turn[which, p].reshape(height * chans, width))
+            ref[:, p] = moved.reshape(chans, height, width).astype(BF)
+
     def dec_row(q, _):
         k = 18 * chans
         out = conv_row(wd[...], [js[p, pl.ds(q, 3)].reshape(k, width) for p in range(depth + 2)], depth)
         for p in range(depth):
-            dec_out[p, q] = out[p].astype(BF)
+            turn[0, p, q] = out[p].astype(BF)
 
     lax.fori_loop(0, height // 2, dec_row, None)
 
     second = advance(first, 0)
     lax.fori_loop(height // 2, height, dec_row, None)
+    channels_first(0, dec_out)
     landed(ecopies, recvs)
 
     def fill_enc(y, _):
@@ -449,15 +546,16 @@
         k = 9 * chans
         out = conv_row(web[...], [es[p, pl.ds(q, 3)].reshape(k, width) for p in range(depth + 2)], depth)
         for p in range(depth):
-            vg_out[p, q] = out[p].astype(BF)
+            turn[1, p, q] = out[p].astype(BF)
 
     third = advance(second, 1)
     lax.fori_loop(0, height // 2, vol_row, None)
     fourth = advance(third, 2)
     lax.fori_loop(height // 2, height, vol_row, None)
+    channels_first(1, vg_out)
     for c in fourth[1]:
         c.wait_recv()
-    sum_out[...] = ar[3, 0:groups[0][0]].astype(F32).reshape(sum_out.shape)
+    sum_out[...] = ar[3, 0:groups[0][0]].reshape(sum_out.shape)
 
     left(zcopies, esends)
     for copies in (vcopies, pcopies, gcopies, ucopies, scopies, ecopies):
@@ -465,15 +563,6 @@
     for copies in (first, second, third, fourth):
         for c in copies[0]:
             c.wait_send()
-
-
-def stacked(weight):
-    k = 9 * weight.shape[1]
-    return jnp.swapaxes(weight.reshape(3, k, weight.shape[2]), 1, 2).reshape(3 * weight.shape[2], k)
-
-
-def flipped(weight):
-    return jnp.transpose(weight[::-1], (0, 2, 1))
 
 
 def per_device(sizes, volume, enc_weight, coarse_weight, up_weight, dec_weight, cotangent):
@@ -484,12 +573,22 @@
     per = -(-18 // owners)
     pair = jnp.transpose(jnp.concatenate([volume, cotangent], axis=0), (1, 2, 0, 3))
     operands = (
-        pair, stacked(enc_weight), stacked(dec_weight), stacked(flipped(dec_weight)),
-        stacked(coarse_weight), stacked(flipped(coarse_weight)), stacked(flipped(enc_weight)),
-        up_weight.T, up_weight)
+        pair, jnp.transpose(enc_weight, (1, 2, 0)), coarse_weight, up_weight.T, jnp.transpose(dec_weight, (0, 2, 1)))
     c2 = 2 * chans
     widest = max(owners, nx * ny // owners, nz) - 1
     scratch = [
+        ((16, 16, 27), BF),
+        ((27, 16, 32), BF),
+        ((16, 32), BF),
+        ((27, 16, 32), BF),
+        ((48, 144), BF),
+        ((48, 288), BF),
+        ((96, 144), BF),
+        ((96, 144), BF),
+        ((48, 288), BF),
+        ((48, 144), BF),
+        ((32, 16), BF),
+        ((2, d, h, chans, w), BF),
         ((d + 2, h + 2, c2, w), BF),
         ((2, d, chans, w), BF),
         ((2, 3, d + 2, chans, w), BF),
@@ -514,33 +613,32 @@
         ((4, widest + 1, per, 16, w), BF),
     ]
     dma = pltpu.SemaphoreType.DMA
-    sems = [dma((8,))] * 2 + [dma((18,))] * 2 + [dma((8,))] * 10 + [dma((4, max(widest, 1)))] * 2
+    sems = [dma((8,))] * 2 + [dma((18,))] * 2 + [dma((8,))] * 10 + [dma((4, max(widest, 1)))] * 2 + [dma((4,))]
+    hbm = pl.BlockSpec(memory_space=pl.ANY)
     vmem = pl.BlockSpec(memory_space=pltpu.VMEM)
     dec, vg, total = pl.pallas_call(
         functools.partial(kernel, sizes),
         out_shape=(
-            jax.ShapeDtypeStruct((d, h, chans, w), BF),
-            jax.ShapeDtypeStruct((d, h, chans, w), BF),
-            jax.ShapeDtypeStruct((owners * per, 16, w), F32)),
-        in_specs=[vmem] * len(operands),
+            jax.ShapeDtypeStruct((chans, d, h, w), BF),
+            jax.ShapeDtypeStruct((chans, d, h, w), BF),
+            jax.ShapeDtypeStruct((owners * per, 16, w), BF)),
+        in_specs=[vmem] + [hbm] * 4,
         out_specs=(vmem,) * 3,
         scratch_shapes=[pltpu.VMEM(s, t) for s, t in scratch] + sems,
         compiler_params=pltpu.CompilerParams(
             collective_id=0, has_side_effects=True, vmem_limit_bytes=48 * 1024 * 1024),
     )(*operands)
-    g = total[:18].reshape(288, w)
-    tail = g[240:288]
-    enc = jnp.transpose(g[0:48].reshape(48, 8, 16), (1, 0, 2)).reshape(24, 16, 16)
-    enc = jnp.concatenate([enc, tail[:, 0:16].reshape(3, 16, 16)], axis=0)
-    halves = []
-    for first, lane in ((48, 16), (96, 32)):
-        half = jnp.transpose(g[first:first + 48].reshape(48, 8, 16), (1, 0, 2)).reshape(24, 16, 16)
-        halves.append(jnp.concatenate([half, tail[:, lane:lane + 16].reshape(3, 16, 16)], axis=0))
-    decg = jnp.concatenate(halves, axis=1)
-    coarse = jnp.transpose(g[144:240].reshape(2, 48, 4, 32), (0, 2, 1, 3)).reshape(24, 16, 32)
-    coarse = jnp.concatenate([coarse, tail[:, 64:96].reshape(3, 16, 32)], axis=0)
-    upg = tail[0:32, 48:64]
-    return (jnp.transpose(dec, (2, 0, 1, 3)), jnp.transpose(vg, (2, 0, 1, 3)), enc, coarse, upg, decg)
+    grads = ((16, 16, 27), (27, 16, 32), (16, 32), (27, 16, 32))
+    dec, vg, enc, coarse, upg, decg = pl.pallas_call(
+        finish,
+        out_shape=tuple(jax.ShapeDtypeStruct(x.shape, BF) for x in (dec, vg))
+        + tuple(jax.ShapeDtypeStruct(x, F32) for x in grads),
+        in_specs=[vmem] * 3,
+        out_specs=(hbm,) * 6,
+        scratch_shapes=[pltpu.VMEM(x, F32) for x in grads] + [dma((6,))],
+        compiler_params=pltpu.CompilerParams(vmem_limit_bytes=8 * 1024 * 1024),
+    )(dec, vg, total)
+    return (dec, vg, jnp.transpose(enc, (2, 0, 1)), coarse, upg.T, jnp.transpose(decg, (0, 2, 1)))
 
 
 def solution(mesh):

time: 81 us -> 72.8 us (0.90)
  local copies, waits for them, and re-layouts: 10.9 us -> 1.95 us
  Pallas kernels: 68.1 us -> 70 us
  other arithmetic: 0.88 us -> 0.02 us
    unnamed x20 -> x12, local copies, waits for them, and re-layouts: 8.05 us -> 1.95 us
    reshape x16 -> x0, local copies, waits for them, and re-layouts: 1.88 us -> none  [the longest x6 0.82 us: stacked(): weight.reshape(3, k, weight.shape[2])]
    pallas_call x0 -> x1, Pallas kernels: none -> 1.48 us  [per_device(): pl.pallas_call(finish, out_shape=tuple((jax.ShapeDtypeStruct(x.shape, BF)...]
    concatenate x3 -> x0, other arithmetic: 0.86 us -> none  [the longest x1 0.7 us: per_device(): jnp.concatenate([coarse, tail[:, 64:96].reshape(3, 16, 32)], axis=0)]
where the time goes in v4:
time: 72.8 us; the launch traced here: 72.7 us
  Pallas kernels  70 us (96%)
  local copies, waits for them, and re-layouts  1.95 us (3%)
    pallas_call x1, Pallas kernels, per_device(): pl.pallas_call(functools.partial(kernel, sizes), out_shape=(jax.ShapeDtyp...  68.5 us
    unnamed x12, local copies, waits for them, and re-layouts  1.95 us
    pallas_call x1, Pallas kernels, per_device(): pl.pallas_call(finish, out_shape=tuple((jax.ShapeDtypeStruct(x.shape, BF)...  1.48 us

profile of v4, /device:TPU:1, one launch (start us, length us, event | category | flops | bytes accessed | tf_op | source)
XLA Modules:
  0.0 72.7 jit_solution(3782634097493858820)
XLA Ops:
  0.6 0.0 copy-start.4
  0.6 1.0 %copy.12 = bf16[16,4,8,128]{3,0,2,1:T(8,128)(2,1)S(1)} copy(bf16[16,4,8,128]{3,2,1,0:T(8,128)(2,1)} %param.6) | data formatting | bytes 262144 | tf_op args[0]
  1.6 0.0 copy-done.4
  1.6 0.1 copy.13
  1.7 0.0 copy-start
  1.7 0.0 copy-start.1
  1.7 0.0 copy-start.2
  1.7 0.0 copy-start.3
  1.8 0.8 %copy-done = bf16[27,16,32]{2,1,0:T(8,128)(2,1)S(1)} copy-done((bf16[27,16,32]{2,1,0:T(8,128)(2,1)S(1)}, bf16[27,16,32]{2,1,0:T(8,128)(2,1)}, u32[]{:S(2)}) %copy-start) | copy-done | bytes 27672
  2.6 0.1 copy-done.1
  2.7 0.0 copy-done.2
  2.7 0.0 copy-done.3
  2.7 68.5 %shard_map.109 = (bf16[16,4,8,128]{3,2,1,0:T(8,128)(2,1)S(1)}, bf16[16,4,8,128]{3,2,1,0:T(8,128)(2,1)S(1)}, bf16[24,16,128]{2,1,0:T(8,128)(2,1)S(1)}) custom-call(bf16[4,8,32,128]{3,2,1,0:T(8,128)(2,1)S(1)} %maximum_bitcast_fusion.vc, bf16[16,16,27]{2,1,0:T(8,128)(2,1)S(1)} %bitcast.9, bf16[27,16,32]{2,1,0:T(8,128)(2,1)S(1)} %copy-done, ...), custom_call_target="tpu_custom_call" | custom-call | tf_op jit(solution)/shard_map/pallas_call | solution.py:619
  71.2 1.5 %shard_map.110 = (bf16[16,4,8,128]{3,2,1,0:T(8,128)(2,1)}, bf16[16,4,8,128]{3,2,1,0:T(8,128)(2,1)}, f32[16,16,27]{2,1,0:T(8,128)}, f32[27,16,32]{2,1,0:T(8,128)}...) custom-call(bf16[16,4,8,128]{3,2,1,0:T(8,128)(2,1)S(1)} %get-tuple-element.15.dec, ...), custom_call_target="tpu_custom_call" | custom-call | tf_op jit(solution)/shard_map/pallas_call | solution.py:632
  (1 shorter events, 0.0 us)
Async XLA Ops:
  0.6 1.0 %copy-start.4 = (bf16[16,4,8,128]{3,2,1,0:T(8,128)(2,1)S(1)}, bf16[16,4,8,128]{3,2,1,0:T(8,128)(2,1)}, u32[]{:S(2)}) copy-start(bf16[16,4,8,128]{3,2,1,0:T(8,128)(2,1)} %param.11) | copy-start | bytes 393220
  1.7 0.9 %copy-start = (bf16[27,16,32]{2,1,0:T(8,128)(2,1)S(1)}, bf16[27,16,32]{2,1,0:T(8,128)(2,1)}, u32[]{:S(2)}) copy-start(bf16[27,16,32]{2,1,0:T(8,128)(2,1)} %coarse_in.1) | copy-start | bytes 82948
  1.7 0.9 %copy-start.1 = (bf16[27,32,16]{1,2,0:T(8,128)(2,1)S(1)}, bf16[27,32,16]{1,2,0:T(8,128)(2,1)}, u32[]{:S(2)}) copy-start(bf16[27,32,16]{1,2,0:T(8,128)(2,1)} %param.10) | copy-start | bytes 82948
  1.7 0.9 %copy-start.2 = (bf16[27,16,16]{0,2,1:T(8,128)(2,1)S(1)}, bf16[27,16,16]{0,2,1:T(8,128)(2,1)}, u32[]{:S(2)}) copy-start(bf16[27,16,16]{0,2,1:T(8,128)(2,1)} %param.7) | copy-start | bytes 41476
  1.7 0.9 %copy-start.3 = (bf16[32,16]{0,1:T(8,128)(2,1)S(1)}, bf16[32,16]{0,1:T(8,128)(2,1)}, u32[]{:S(2)}) copy-start(bf16[32,16]{0,1:T(8,128)(2,1)} %param.9) | copy-start | bytes 3076

commit v5 on v4

--- a/solution.py
+++ b/solution.py
@@ -11,7 +11,7 @@
 BF = jnp.bfloat16
 F32 = jnp.float32
 MESH = pl.DeviceIdType.MESH
-DIRS = tuple((dx, dy) for dx in (-1, 0, 1) for dy in (-1, 0, 1) if (dx, dy) != (0, 0))
+DIRS = tuple((dx, dy) for dy in (-1, 1, 0) for dx in (-1, 1, 0) if (dx, dy) != (0, 0))
 
 
 def dot(a, b):
@@ -143,7 +143,7 @@
 
     sends = [all_of(exists(dx, ix, nx), exists(dy, iy, ny)) for dx, dy in DIRS]
     recvs = [all_of(exists(-dx, ix, nx), exists(-dy, iy, ny)) for dx, dy in DIRS]
-    ends = tuple((dx, dy, s) for s in (-1, 1) for dx in (-1, 0, 1) for dy in (-1, 0, 1))
+    ends = tuple((dx, dy, s) for dy in (-1, 1, 0) for dx in (-1, 1, 0) for s in (-1, 1))
     esends = [all_of(exists(dx, ix, nx), exists(dy, iy, ny), exists(dz, iz, nz)) for dx, dy, dz in ends]
     erecvs = [all_of(exists(-dx, ix, nx), exists(-dy, iy, ny), exists(-dz, iz, nz)) for dx, dy, dz in ends]
 
@@ -214,6 +214,10 @@
         for c, r in zip(copies, conds):
             guarded(r, c.wait_recv)
 
+    def landed_rows(copies, conds, dirs, rim):
+        part = [i for i, d in enumerate(dirs) if (d[1] != 0) == rim]
+        landed([copies[i] for i in part], [conds[i] for i in part])
+
     def left(copies, conds):
         for c, s in zip(copies, conds):
             guarded(s, c.wait_send)
@@ -247,8 +251,6 @@
     for c in loads:
         c.wait()
     arrange_weights(enc_w, coarse_w, upt, dec_w, we, wd, wdb, wc, wcb, web, up)
-    landed(vcopies, recvs)
-    landed(zcopies, erecvs)
 
     def shifted(wide, c):
         if c == 1:
@@ -269,7 +271,6 @@
             for c in range(3):
                 ref[:, y, c] = shifted(wide, c).astype(BF).reshape(depth + 2, chans, 2 * width)
 
-    lax.fori_loop(0, height + 2, fill_inputs, None)
 
     fine = lax.broadcasted_iota(jnp.int32, (1, 2 * width), 1)
     coarse = lax.broadcasted_iota(jnp.int32, (1, width), 1)
@@ -293,7 +294,16 @@
             skip[1 + p, 1 + q] = (t * sig * fine_mask).astype(BF)
             slope[p, q] = sig * (1.0 + t * (1.0 - sig)) * fine_mask
 
-    lax.fori_loop(0, height, enc_row, None)
+    landed_rows(zcopies, erecvs, ends, False)
+    landed_rows(vcopies, recvs, DIRS, False)
+    lax.fori_loop(1, height + 1, fill_inputs, None)
+    lax.fori_loop(1, height - 1, enc_row, None)
+    landed_rows(zcopies, erecvs, ends, True)
+    landed_rows(vcopies, recvs, DIRS, True)
+    for y in (0, height + 1):
+        fill_inputs(y, None)
+    for q in (0, height - 1):
+        enc_row(q, None)
 
     pool = (lax.broadcasted_iota(jnp.int32, (2 * width, width), 0) // 2
             == lax.broadcasted_iota(jnp.int32, (2 * width, width), 1)).astype(BF)
@@ -326,15 +336,14 @@
     grad = dot(ughi[...].reshape(flat), pool) + dot(uglo[...].reshape(flat), pool)
     ug[...] = grad.astype(BF).reshape(ug.shape)
 
-    landed(pcopies, recvs)
-
     def fill_pooled(q, _):
         wide = ph[:, q].reshape((cd + 2) * chans, width).astype(F32)
         for c in range(3):
             ps[:, q, c] = shifted(wide, c).astype(BF).reshape(cd + 2, chans, width)
 
-    lax.fori_loop(0, ch + 2, fill_pooled, None)
-    for q in range(ch):
+    landed_rows(pcopies, recvs, DIRS, False)
+    lax.fori_loop(1, ch + 1, fill_pooled, None)
+    def coarse_row(q):
         k = 9 * chans
         pre = conv_row(wc[...], [ps[p, q:q + 3].reshape(k, width) for p in range(cd + 2)], cd)
         for p in range(cd):
@@ -346,6 +355,13 @@
             back = dot(up[...], ug[p, q])
             gh[1 + p, 1 + q] = (back * (sig * (1.0 + t * (1.0 - sig)) * coarse_mask)).astype(BF)
 
+    for q in range(1, ch - 1):
+        coarse_row(q)
+    landed_rows(pcopies, recvs, DIRS, True)
+    for q in (0, ch + 1):
+        fill_pooled(q, None)
+    for q in (0, ch - 1):
+        coarse_row(q)
     gcopies = exchange(gh, rim_src(1, cd, ch, 1), gh, rim_dst(1, cd, ch), gsend, grecv)
     begin(gcopies, sends)
     ucopies = exchange(uh, rim_src(1, cd, ch, 1), uh, rim_dst(1, cd, ch), usend, urecv)
@@ -427,14 +443,14 @@
     total, last = joined_taps(0)
     put(48, total)
     tail = jnp.where(group16 == 1, last, tail)
-    landed(gcopies, recvs)
 
     def fill_coarse(y, _):
         wide = gh[:, y].reshape((cd + 2) * 2 * chans, width).astype(F32)
         for c in range(3):
             gs[:, y, c] = shifted(wide, c).astype(BF).reshape(cd + 2, 2 * chans, width)
 
-    lax.fori_loop(0, ch + 2, fill_coarse, None)
+    landed_rows(gcopies, recvs, DIRS, False)
+    lax.fori_loop(1, ch + 1, fill_coarse, None)
     spread = (lax.broadcasted_iota(jnp.int32, (width, 2 * width), 1) // 2
               == lax.broadcasted_iota(jnp.int32, (width, 2 * width), 0)).astype(BF)
 
@@ -451,7 +467,12 @@
                     g = (jg[2 * p + e, 2 * q + f] + wide) * slope[2 * p + e, 2 * q + f]
                     eh[1 + 2 * p + e, 1 + 2 * q + f] = g.astype(BF)
 
-    lax.fori_loop(0, ch, back_row, None)
+    lax.fori_loop(1, ch - 1, back_row, None)
+    landed_rows(gcopies, recvs, DIRS, True)
+    for y in (0, ch + 1):
+        fill_coarse(y, None)
+    for q in (0, ch - 1):
+        back_row(q, None)
     ecopies = exchange(eh, rim_src(1, depth, height, 1), eh, rim_dst(1, depth, height), esend, erecv)
     begin(ecopies, sends)
 
@@ -485,7 +506,7 @@
     def ring(phase):
         count, me, member = groups[phase % 3]
         out, got = [], []
-        for k in range(1, count):
+        for k in sorted(range(1, count), key=lambda k: abs(2 * k - count)):
             to = lax.rem(me + k, count)
             frm = lax.rem(me - k + count, count)
             src = gr.at[pl.ds(to * per, per)] if phase == 0 else ar.at[phase, me]

time: 72.8 us -> 66.2 us (0.909)
  Pallas kernels: 70 us -> 63.4 us
    pallas_call x1, Pallas kernels: 68.5 us -> 61.9 us  [per_device(): pl.pallas_call(functools.partial(kernel, sizes), out_shape=(jax.ShapeDtyp...]
where the time goes in v5:
time: 66.2 us; the launch traced here: 66.1 us
  Pallas kernels  63.4 us (96%)
  local copies, waits for them, and re-layouts  1.95 us (3%)
  between operations  0.7 us (1%)
    pallas_call x1, Pallas kernels, per_device(): pl.pallas_call(functools.partial(kernel, sizes), out_shape=(jax.ShapeDtyp...  61.9 us
    unnamed x12, local copies, waits for them, and re-layouts  1.95 us
    pallas_call x1, Pallas kernels, per_device(): pl.pallas_call(finish, out_shape=tuple((jax.ShapeDtypeStruct(x.shape, BF)...  1.48 us

profile of v5, /device:TPU:1, one launch (start us, length us, event | category | flops | bytes accessed | tf_op | source)
XLA Modules:
  0.0 66.1 jit_solution(9319115247511768925)
XLA Ops:
  0.6 0.0 copy-start.4
  0.6 1.0 %copy.12 = bf16[16,4,8,128]{3,0,2,1:T(8,128)(2,1)S(1)} copy(bf16[16,4,8,128]{3,2,1,0:T(8,128)(2,1)} %param.6) | data formatting | bytes 262144 | tf_op args[0]
  1.6 0.0 copy-done.4
  1.6 0.1 copy.13
  1.7 0.0 copy-start
  1.7 0.0 copy-start.1
  1.7 0.0 copy-start.2
  1.7 0.0 copy-start.3
  1.8 0.8 %copy-done = bf16[27,16,32]{2,1,0:T(8,128)(2,1)S(1)} copy-done((bf16[27,16,32]{2,1,0:T(8,128)(2,1)S(1)}, bf16[27,16,32]{2,1,0:T(8,128)(2,1)}, u32[]{:S(2)}) %copy-start) | copy-done | bytes 27672
  2.6 0.1 copy-done.1
  2.7 0.0 copy-done.2
  2.7 0.0 copy-done.3
  2.7 61.9 %shard_map.109 = (bf16[16,4,8,128]{3,2,1,0:T(8,128)(2,1)S(1)}, bf16[16,4,8,128]{3,2,1,0:T(8,128)(2,1)S(1)}, bf16[24,16,128]{2,1,0:T(8,128)(2,1)S(1)}) custom-call(bf16[4,8,32,128]{3,2,1,0:T(8,128)(2,1)S(1)} %maximum_bitcast_fusion.vc, bf16[16,16,27]{2,1,0:T(8,128)(2,1)S(1)} %bitcast.9, bf16[27,16,32]{2,1,0:T(8,128)(2,1)S(1)} %copy-done, ...), custom_call_target="tpu_custom_call" | custom-call | tf_op jit(solution)/shard_map/pallas_call | solution.py:640
  64.6 1.5 %shard_map.110 = (bf16[16,4,8,128]{3,2,1,0:T(8,128)(2,1)}, bf16[16,4,8,128]{3,2,1,0:T(8,128)(2,1)}, f32[16,16,27]{2,1,0:T(8,128)}, f32[27,16,32]{2,1,0:T(8,128)}...) custom-call(bf16[16,4,8,128]{3,2,1,0:T(8,128)(2,1)S(1)} %get-tuple-element.15.dec, ...), custom_call_target="tpu_custom_call" | custom-call | tf_op jit(solution)/shard_map/pallas_call | solution.py:653
  (1 shorter events, 0.0 us)
Async XLA Ops:
  0.6 1.0 %copy-start.4 = (bf16[16,4,8,128]{3,2,1,0:T(8,128)(2,1)S(1)}, bf16[16,4,8,128]{3,2,1,0:T(8,128)(2,1)}, u32[]{:S(2)}) copy-start(bf16[16,4,8,128]{3,2,1,0:T(8,128)(2,1)} %param.11) | copy-start | bytes 393220
  1.7 0.9 %copy-start = (bf16[27,16,32]{2,1,0:T(8,128)(2,1)S(1)}, bf16[27,16,32]{2,1,0:T(8,128)(2,1)}, u32[]{:S(2)}) copy-start(bf16[27,16,32]{2,1,0:T(8,128)(2,1)} %coarse_in.1) | copy-start | bytes 82948
  1.7 0.9 %copy-start.1 = (bf16[27,32,16]{1,2,0:T(8,128)(2,1)S(1)}, bf16[27,32,16]{1,2,0:T(8,128)(2,1)}, u32[]{:S(2)}) copy-start(bf16[27,32,16]{1,2,0:T(8,128)(2,1)} %param.10) | copy-start | bytes 82948
  1.7 0.9 %copy-start.2 = (bf16[27,16,16]{0,2,1:T(8,128)(2,1)S(1)}, bf16[27,16,16]{0,2,1:T(8,128)(2,1)}, u32[]{:S(2)}) copy-start(bf16[27,16,16]{0,2,1:T(8,128)(2,1)} %param.7) | copy-start | bytes 41476
  1.7 0.9 %copy-start.3 = (bf16[32,16]{0,1:T(8,128)(2,1)S(1)}, bf16[32,16]{0,1:T(8,128)(2,1)}, u32[]{:S(2)}) copy-start(bf16[32,16]{0,1:T(8,128)(2,1)} %param.9) | copy-start | bytes 3076

commit v6 on v5

--- a/solution.py
+++ b/solution.py
@@ -55,46 +55,46 @@
     up[...] = dot_tn(upt[...], zero_one((16, 16), lambda r, l: r == l).astype(BF)).astype(BF)
 
 
-def finish(dec, vg, total, dec_out, vg_out, enc_out, coarse_out, up_out, decg_out,
+def finish(split, dec, vg, total, dec_out, vg_out, enc_out, coarse_out, up_out, decg_out,
            enc, coarse, up, decg, sems):
     copies = [pltpu.make_async_copy(a, b, sems.at[k]) for k, (a, b) in enumerate(
         ((dec, dec_out), (vg, vg_out), (enc, enc_out), (coarse, coarse_out), (up, up_out), (decg, decg_out)))]
     copies[0].start()
     copies[1].start()
 
-    def rows(first, count):
-        return total[first // 16:(first + count) // 16].reshape(count, 128)
+    def tile(which, k):
+        return total[which * split + k]
 
     eye = zero_one((128, 128), lambda r, l: r == l).astype(BF)
     for c in range(3):
-        last = rows(240 + 16 * c, 16)
-        block = jnp.concatenate([rows(48 + 16 * c, 16), rows(96 + 16 * c, 16)], axis=0)
+        block = jnp.concatenate([tile(0, 6 + c), tile(1, 3 + c)], axis=0)
         turned = dot_nt(eye, block).reshape(8, 16, 32)
         for g in range(8):
             decg[3 * g + c] = turned[g]
-        skip_last = dot_nt(zero_one((16, 128), lambda r, l: l == 16 + r).astype(BF), last)
-        upper_last = dot_nt(zero_one((16, 128), lambda r, l: l == 32 + r).astype(BF), last)
+        skip_last = dot_nt(zero_one((16, 128), lambda r, l: l == 16 * c + r).astype(BF), tile(0, 10))
+        upper_last = dot_nt(zero_one((16, 128), lambda r, l: l == 48 + 16 * c + r).astype(BF), tile(1, 6))
         decg[24 + c] = jnp.concatenate([skip_last, upper_last], axis=1)
     copies[5].start()
     for c in range(3):
         for half in range(2):
-            block = rows(144 + 48 * half + 16 * c, 16)
+            block = tile(0, 3 * half + c)
             for g in range(4):
                 pick = zero_one((128, 32), lambda r, l: r == 32 * g + l).astype(BF)
                 coarse[3 * (4 * half + g) + c] = dot(block, pick)
-        pick = zero_one((128, 32), lambda r, l: r == 64 + l).astype(BF)
-        coarse[24 + c] = dot(rows(240 + 16 * c, 16), pick)
+        pick = zero_one((128, 32), lambda r, l: r == 32 * c + l).astype(BF)
+        coarse[24 + c] = dot(tile(0, 9), pick)
     copies[3].start()
-    up[...] = dot_nt(zero_one((16, 128), lambda r, l: l == 48 + r).astype(BF), rows(240, 32))
+    up[...] = jnp.concatenate(
+        [dot_nt(zero_one((16, 128), lambda r, l: l == 96 + 16 * k + r).astype(BF), tile(0, 9)) for k in range(2)], axis=1)
     copies[4].start()
     grow = zero_one((256, 16), lambda r, l: l == r // 16).astype(BF)
     same = zero_one((256, 128), lambda r, l: r % 16 == l % 16)
     flat = jnp.zeros((256, 27), F32)
     for c in range(3):
-        wide = jnp.where(same, dot(grow, rows(16 * c, 16)), 0.0).astype(BF)
+        wide = jnp.where(same, dot(grow, tile(1, c)), 0.0).astype(BF)
         flat = flat + dot(wide, zero_one((128, 27), lambda r, l: l == 3 * (r // 16) + c).astype(BF))
-        wide = jnp.where(same, dot(grow, rows(240 + 16 * c, 16)), 0.0).astype(BF)
-        flat = flat + dot(wide, zero_one((128, 27), lambda r, l: (r < 16) & (l == 24 + c)).astype(BF))
+        wide = jnp.where(same, dot(grow, tile(1, 6)), 0.0).astype(BF)
+        flat = flat + dot(wide, zero_one((128, 27), lambda r, l: (r // 16 == c) & (l == 24 + c)).astype(BF))
     enc[...] = flat.reshape(16, 16, 27)
     copies[2].start()
     for c in copies:
@@ -120,9 +120,9 @@
 def kernel(sizes, vc, enc_in, coarse_in, upt_in, dec_in, dec_out, vg_out, sum_out,
            enc_w, coarse_w, upt, dec_w, we, wd, wdb, wc, wcb, web, up, turn,
            vct, pk, er, vs, cs, skip, slope, jg, ughi, uglo, ug, ph, ps, act, uh, gh, gs, js, eh, es,
-           gr, ar,
+           gr0, gr1, ar0, ar1,
            vsend, vrecv, zsend, zrecv, psend, precv, gsend, grecv, usend, urecv, ssend, srecv, esend, erecv,
-           asend, arecv, wsem):
+           asend0, arecv0, asend1, arecv1, wsem):
     nx, ny, nz = sizes
     ix, iy, iz = (lax.axis_index(a) for a in AXES)
     depth, height, _, width = vc.shape
@@ -272,6 +272,44 @@
                 ref[:, y, c] = shifted(wide, c).astype(BF).reshape(depth + 2, chans, 2 * width)
 
 
+    sets = ((gr0, ar0, asend0, arecv0), (gr1, ar1, asend1, arecv1))
+
+    def ring(which, phase):
+        gr, ar, asend, arecv = sets[which]
+        count, me, member = groups[phase % 3]
+        per = gr.shape[0] // groups[0][0]
+        out, got = [], []
+        for k in sorted(range(1, count), key=lambda k: abs(2 * k - count)):
+            to = lax.rem(me + k, count)
+            frm = lax.rem(me - k + count, count)
+            src = gr.at[pl.ds(to * per, per)] if phase == 0 else ar.at[phase, me]
+
+            def copy(slot):
+                return pltpu.make_async_remote_copy(
+                    src_ref=src, dst_ref=ar.at[phase, slot], send_sem=asend.at[phase, k - 1],
+                    recv_sem=arecv.at[phase, k - 1], device_id=member(to), device_id_type=MESH)
+
+            out.append(copy(me))
+            got.append(copy(frm))
+        for c in out:
+            c.start()
+        if phase == 0:
+            ar[0, me] = gr[pl.ds(me * per, per)]
+        everything.extend(out)
+        return got
+
+    everything = []
+
+    def advance(which, copies, phase):
+        ar = sets[which][1]
+        for c in copies:
+            c.wait_recv()
+        total = ar[phase, 0].astype(F32)
+        for k in range(1, groups[phase][0]):
+            total = total + ar[phase, k].astype(F32)
+        ar[phase + 1, groups[(phase + 1) % 3][1]] = total.astype(BF)
+        return ring(which, phase + 1)
+
     fine = lax.broadcasted_iota(jnp.int32, (1, 2 * width), 1)
     coarse = lax.broadcasted_iota(jnp.int32, (1, width), 1)
     low_ok = jnp.where(iz > 0, 1.0, 0.0).astype(F32)
@@ -383,10 +421,19 @@
             out.append(total)
         return out
 
-    def put(first, value):
-        gr[first // 16:first // 16 + 3] = value.astype(BF).reshape(3, 16, width)
-
-    tail = jnp.zeros((3 * chans, width), F32)
+    def put(ref, first, value):
+        tiles = value.shape[0] // 16
+        ref[first:first + tiles] = value.astype(BF).reshape(tiles, 16, width)
+
+    def place(total, gid, first, block):
+        for k in range(block.shape[0] // 16):
+            total = jnp.where(gid == first + k, block[16 * k:16 * k + 16], total)
+        return total
+
+    for ref, used in ((gr0, 11), (gr1, 7)):
+        if ref.shape[0] > used:
+            ref[used:] = jnp.zeros((ref.shape[0] - used, 16, width), BF)
+    blank = jnp.zeros((16, width), F32)
     step = 3 * chans
     taps = []
     masked = [jnp.where(own_coarse, gh[1 + p, 1:1 + ch].reshape(2 * chans * ch, width), 0)
@@ -398,15 +445,15 @@
         total = jnp.zeros((step, width), F32)
         for g in range(4):
             total = jnp.where(group32 == g, taps[4 * half + g], total)
-        put(144 + 48 * half, total)
-    tail = jnp.where(group32 == 2, taps[8], tail)
+        put(gr0, 3 * half, total)
+    side = place(blank, group32, 0, taps[8])
     up_total = jnp.zeros((2 * chans, width), F32)
     for p in range(cd):
         for q in range(ch):
             g = jnp.where(own_coarse, ug[p, q], 0)
             up_total = up_total + dot_nt(act[p, q], jnp.concatenate([g] * 8, axis=0))
-    up_total = jnp.concatenate([up_total, jnp.zeros((chans, width), F32)], axis=0)
-    tail = jnp.where(group16 == 3, up_total, tail)
+    side = place(side, group16, 6, up_total)
+    put(gr0, 9, side)
 
     def fill_skip(first, count, y):
         wide = skip[first:first + count, y].reshape(count * chans, 2 * width).astype(F32)
@@ -441,8 +488,9 @@
             [vc[p, :, chans:2 * chans].reshape(height * chans, width) for p in range(depth)])
 
     total, last = joined_taps(0)
-    put(48, total)
-    tail = jnp.where(group16 == 1, last, tail)
+    put(gr0, 6, total)
+    put(gr0, 10, place(blank, group16, 0, last))
+    early = ring(0, 0)
 
     def fill_coarse(y, _):
         wide = gh[:, y].reshape((cd + 2) * 2 * chans, width).astype(F32)
@@ -475,6 +523,7 @@
         back_row(q, None)
     ecopies = exchange(eh, rim_src(1, depth, height, 1), eh, rim_dst(1, depth, height), esend, erecv)
     begin(ecopies, sends)
+    early = advance(0, early, 0)
 
     landed(ucopies, recvs)
     low = lax.broadcasted_iota(jnp.int32, (width, width), 0)
@@ -489,50 +538,15 @@
                 js[x, y, c, chans:2 * chans] = wide[(x + 1) // 2, (y + 1) // 2]
 
     total, last = joined_taps(chans)
-    put(96, total)
-    tail = jnp.where(group16 == 2, last, tail)
+    put(gr1, 3, total)
+    side = place(blank, group16, 3, last)
     total, last = fine_taps(
         lambda x: vs[x, :, :, :, 0:width].reshape((height + 2) * 3 * chans, width), 3 * chans,
         [eh[1 + p, 1:1 + height, :, 0:width].reshape(height * chans, width) for p in range(depth)])
-    put(0, total)
-    tail = jnp.where(group16 == 0, last, tail)
-    put(240, tail)
-    used = 288 // 16
-    if gr.shape[0] > used:
-        gr[used:] = jnp.zeros((gr.shape[0] - used, 16, width), BF)
-
-    per = gr.shape[0] // groups[0][0]
-
-    def ring(phase):
-        count, me, member = groups[phase % 3]
-        out, got = [], []
-        for k in sorted(range(1, count), key=lambda k: abs(2 * k - count)):
-            to = lax.rem(me + k, count)
-            frm = lax.rem(me - k + count, count)
-            src = gr.at[pl.ds(to * per, per)] if phase == 0 else ar.at[phase, me]
-
-            def copy(slot):
-                return pltpu.make_async_remote_copy(
-                    src_ref=src, dst_ref=ar.at[phase, slot], send_sem=asend.at[phase, k - 1],
-                    recv_sem=arecv.at[phase, k - 1], device_id=member(to), device_id_type=MESH)
-
-            out.append(copy(me))
-            got.append(copy(frm))
-        for c in out:
-            c.start()
-        return out, got
-
-    def advance(copies, phase):
-        for c in copies[1]:
-            c.wait_recv()
-        total = ar[phase, 0].astype(F32)
-        for k in range(1, groups[phase][0]):
-            total = total + ar[phase, k].astype(F32)
-        ar[phase + 1, groups[(phase + 1) % 3][1]] = total.astype(BF)
-        return ring(phase + 1)
-
-    first = ring(0)
-    ar[0, groups[0][1]] = gr[pl.ds(groups[0][1] * per, per)]
+    put(gr1, 0, total)
+    put(gr1, 6, place(side, group16, 0, last))
+
+    late = ring(1, 0)
 
     order = zero_one((height * chans, height * chans),
                      lambda r, l: (r // height == l % chans) & (r % height == l // chans)).astype(BF)
@@ -550,7 +564,8 @@
 
     lax.fori_loop(0, height // 2, dec_row, None)
 
-    second = advance(first, 0)
+    late = advance(1, late, 0)
+    early = advance(0, early, 1)
     lax.fori_loop(height // 2, height, dec_row, None)
     channels_first(0, dec_out)
     landed(ecopies, recvs)
@@ -569,21 +584,22 @@
         for p in range(depth):
             turn[1, p, q] = out[p].astype(BF)
 
-    third = advance(second, 1)
+    late = advance(1, late, 1)
+    early = advance(0, early, 2)
     lax.fori_loop(0, height // 2, vol_row, None)
-    fourth = advance(third, 2)
+    late = advance(1, late, 2)
     lax.fori_loop(height // 2, height, vol_row, None)
     channels_first(1, vg_out)
-    for c in fourth[1]:
+    for c in early + late:
         c.wait_recv()
-    sum_out[...] = ar[3, 0:groups[0][0]].reshape(sum_out.shape)
+    sum_out[0:gr0.shape[0]] = ar0[3, 0:groups[0][0]].reshape(gr0.shape)
+    sum_out[gr0.shape[0]:] = ar1[3, 0:groups[0][0]].reshape(gr1.shape)
 
     left(zcopies, esends)
     for copies in (vcopies, pcopies, gcopies, ucopies, scopies, ecopies):
         left(copies, sends)
-    for copies in (first, second, third, fourth):
-        for c in copies[0]:
-            c.wait_send()
+    for c in everything:
+        c.wait_send()
 
 
 def per_device(sizes, volume, enc_weight, coarse_weight, up_weight, dec_weight, cotangent):
@@ -591,7 +607,7 @@
     chans, d, h, w = volume.shape
     cd, ch = d // 2, h // 2
     owners = min(2, nx) * (ny // 2 if ny > 4 else ny)
-    per = -(-18 // owners)
+    pers = (-(-11 // owners), -(-7 // owners))
     pair = jnp.transpose(jnp.concatenate([volume, cotangent], axis=0), (1, 2, 0, 3))
     operands = (
         pair, jnp.transpose(enc_weight, (1, 2, 0)), coarse_weight, up_weight.T, jnp.transpose(dec_weight, (0, 2, 1)))
@@ -630,11 +646,13 @@
         ((d + 2, h + 2, 3, c2, w), BF),
         ((d + 2, h + 2, chans, 2 * w), BF),
         ((d + 2, h + 2, 3, chans, w), BF),
-        ((owners * per, 16, w), BF),
-        ((4, widest + 1, per, 16, w), BF),
+        ((owners * pers[0], 16, w), BF),
+        ((owners * pers[1], 16, w), BF),
+        ((4, widest + 1, pers[0], 16, w), BF),
+        ((4, widest + 1, pers[1], 16, w), BF),
     ]
     dma = pltpu.SemaphoreType.DMA
-    sems = [dma((8,))] * 2 + [dma((18,))] * 2 + [dma((8,))] * 10 + [dma((4, max(widest, 1)))] * 2 + [dma((4,))]
+    sems = [dma((8,))] * 2 + [dma((18,))] * 2 + [dma((8,))] * 10 + [dma((4, max(widest, 1)))] * 4 + [dma((4,))]
     hbm = pl.BlockSpec(memory_space=pl.ANY)
     vmem = pl.BlockSpec(memory_space=pltpu.VMEM)
     dec, vg, total = pl.pallas_call(
@@ -642,7 +660,7 @@
         out_shape=(
             jax.ShapeDtypeStruct((chans, d, h, w), BF),
             jax.ShapeDtypeStruct((chans, d, h, w), BF),
-            jax.ShapeDtypeStruct((owners * per, 16, w), BF)),
+            jax.ShapeDtypeStruct((owners * sum(pers), 16, w), BF)),
         in_specs=[vmem] + [hbm] * 4,
         out_specs=(vmem,) * 3,
         scratch_shapes=[pltpu.VMEM(s, t) for s, t in scratch] + sems,
@@ -651,7 +669,7 @@
     )(*operands)
     grads = ((16, 16, 27), (27, 16, 32), (16, 32), (27, 16, 32))
     dec, vg, enc, coarse, upg, decg = pl.pallas_call(
-        finish,
+        functools.partial(finish, owners * pers[0]),
         out_shape=tuple(jax.ShapeDtypeStruct(x.shape, BF) for x in (dec, vg))
         + tuple(jax.ShapeDtypeStruct(x, F32) for x in grads),
         in_specs=[vmem] * 3,

time: 66.2 us -> 65.3 us (0.986)
  Pallas kernels: 63.4 us -> 62.5 us
    pallas_call x1, Pallas kernels: 61.9 us -> 61 us  [per_device(): pl.pallas_call(functools.partial(kernel, sizes), out_shape=(jax.ShapeDtyp...]
where the time goes in v6:
time: 65.3 us; the launch traced here: 65.2 us
  Pallas kernels  62.5 us (96%)
  local copies, waits for them, and re-layouts  1.95 us (3%)
  between operations  0.7 us (1%)
    pallas_call x1, Pallas kernels, per_device(): pl.pallas_call(functools.partial(kernel, sizes), out_shape=(jax.ShapeDtyp...  61 us
    unnamed x12, local copies, waits for them, and re-layouts  1.95 us
    pallas_call x1, Pallas kernels, per_device(): pl.pallas_call(functools.partial(finish, owners * pers[0]), out_shape=tup...  1.54 us

profile of v6, /device:TPU:1, one launch (start us, length us, event | category | flops | bytes accessed | tf_op | source)
XLA Modules:
  0.0 65.2 jit_solution(18083569944703193384)
XLA Ops:
  0.6 0.0 copy-start.4
  0.6 1.0 %copy.12 = bf16[16,4,8,128]{3,0,2,1:T(8,128)(2,1)S(1)} copy(bf16[16,4,8,128]{3,2,1,0:T(8,128)(2,1)} %param.6) | data formatting | bytes 262144 | tf_op args[0]
  1.6 0.0 copy-done.4
  1.6 0.1 copy.13
  1.7 0.0 copy-start
  1.7 0.0 copy-start.1
  1.7 0.0 copy-start.2
  1.7 0.0 copy-start.3
  1.8 0.8 %copy-done = bf16[27,16,32]{2,1,0:T(8,128)(2,1)S(1)} copy-done((bf16[27,16,32]{2,1,0:T(8,128)(2,1)S(1)}, bf16[27,16,32]{2,1,0:T(8,128)(2,1)}, u32[]{:S(2)}) %copy-start) | copy-done | bytes 27672
  2.6 0.1 copy-done.1
  2.7 0.0 copy-done.2
  2.7 0.0 copy-done.3
  2.7 61.0 %shard_map.109 = (bf16[16,4,8,128]{3,2,1,0:T(8,128)(2,1)S(1)}, bf16[16,4,8,128]{3,2,1,0:T(8,128)(2,1)S(1)}, bf16[24,16,128]{2,1,0:T(8,128)(2,1)S(1)}) custom-call(bf16[4,8,32,128]{3,2,1,0:T(8,128)(2,1)S(1)} %maximum_bitcast_fusion.vc, bf16[16,16,27]{2,1,0:T(8,128)(2,1)S(1)} %bitcast.9, bf16[27,16,32]{2,1,0:T(8,128)(2,1)S(1)} %copy-done, ...), custom_call_target="tpu_custom_call" | custom-call | tf_op jit(solution)/shard_map/pallas_call | solution.py:658
  63.6 1.5 %shard_map.110 = (bf16[16,4,8,128]{3,2,1,0:T(8,128)(2,1)}, bf16[16,4,8,128]{3,2,1,0:T(8,128)(2,1)}, f32[16,16,27]{2,1,0:T(8,128)}, f32[27,16,32]{2,1,0:T(8,128)}...) custom-call(bf16[16,4,8,128]{3,2,1,0:T(8,128)(2,1)S(1)} %get-tuple-element.15.dec, ...), custom_call_target="tpu_custom_call" | custom-call | tf_op jit(solution)/shard_map/pallas_call | solution.py:671
  (1 shorter events, 0.0 us)
Async XLA Ops:
  0.6 1.0 %copy-start.4 = (bf16[16,4,8,128]{3,2,1,0:T(8,128)(2,1)S(1)}, bf16[16,4,8,128]{3,2,1,0:T(8,128)(2,1)}, u32[]{:S(2)}) copy-start(bf16[16,4,8,128]{3,2,1,0:T(8,128)(2,1)} %param.11) | copy-start | bytes 393220
  1.7 0.9 %copy-start = (bf16[27,16,32]{2,1,0:T(8,128)(2,1)S(1)}, bf16[27,16,32]{2,1,0:T(8,128)(2,1)}, u32[]{:S(2)}) copy-start(bf16[27,16,32]{2,1,0:T(8,128)(2,1)} %coarse_in.1) | copy-start | bytes 82948
  1.7 0.9 %copy-start.1 = (bf16[27,32,16]{1,2,0:T(8,128)(2,1)S(1)}, bf16[27,32,16]{1,2,0:T(8,128)(2,1)}, u32[]{:S(2)}) copy-start(bf16[27,32,16]{1,2,0:T(8,128)(2,1)} %param.10) | copy-start | bytes 82948
  1.7 0.9 %copy-start.2 = (bf16[27,16,16]{0,2,1:T(8,128)(2,1)S(1)}, bf16[27,16,16]{0,2,1:T(8,128)(2,1)}, u32[]{:S(2)}) copy-start(bf16[27,16,16]{0,2,1:T(8,128)(2,1)} %param.7) | copy-start | bytes 41476
  1.7 0.9 %copy-start.3 = (bf16[32,16]{0,1:T(8,128)(2,1)S(1)}, bf16[32,16]{0,1:T(8,128)(2,1)}, u32[]{:S(2)}) copy-start(bf16[32,16]{0,1:T(8,128)(2,1)} %param.9) | copy-start | bytes 3076

commit v7 on v6

--- a/solution.py
+++ b/solution.py
@@ -159,29 +159,26 @@
         (nz, iz, lambda j: (ix, iy, j)),
     )
 
+    barrier = pltpu.get_barrier_semaphore()
+
+    def greet(device):
+        pl.semaphore_signal(barrier, inc=1, device_id=device, device_id_type=MESH)
+
+    for dx, dy, dz in list(ends) + [d + (0,) for d in DIRS]:
+        if dx != 0 or dy != 0:
+            guarded(all_of(exists(dx, ix, nx), exists(dy, iy, ny), exists(dz, iz, nz)),
+                    lambda dx=dx, dy=dy, dz=dz: greet(at(dx, dy, dz)))
+
+    for count, me, member in groups:
+        for k in range(1, count):
+            greet(member(lax.rem(me + k, count)))
+    def both(index, count):
+        return (jnp.where(index > 0, 1, 0) + jnp.where(index < count - 1, 1, 0)).astype(jnp.int32)
+
     loads = [pltpu.make_async_copy(a, b, wsem.at[k]) for k, (a, b) in enumerate(
         ((enc_in, enc_w), (coarse_in, coarse_w), (upt_in, upt), (dec_in, dec_w)))]
     for c in loads:
         c.start()
-
-    for ref in (vct, er, skip, ph, uh, gh, eh):
-        ref[...] = jnp.zeros(ref.shape, ref.dtype)
-    vct[1:1 + depth, 1:1 + height] = vc[...]
-    barrier = pltpu.get_barrier_semaphore()
-
-    def greet(device):
-        pl.semaphore_signal(barrier, inc=1, device_id=device, device_id_type=MESH)
-
-    for count, me, member in groups:
-        for k in range(1, count):
-            greet(member(lax.rem(me + k, count)))
-    for dx, dy, dz in [d + (0,) for d in DIRS] + list(ends):
-        if dx != 0 or dy != 0:
-            guarded(all_of(exists(dx, ix, nx), exists(dy, iy, ny), exists(dz, iz, nz)),
-                    lambda dx=dx, dy=dy, dz=dz: greet(at(dx, dy, dz)))
-
-    def both(index, count):
-        return (jnp.where(index > 0, 1, 0) + jnp.where(index < count - 1, 1, 0)).astype(jnp.int32)
 
     row = lax.broadcasted_iota(jnp.int32, (width, 2 * width), 0)
     lane = lax.broadcasted_iota(jnp.int32, (width, 2 * width), 1)
@@ -248,6 +245,31 @@
             send_sem=zsend.at[d], recv_sem=zrecv.at[d],
             device_id=at(dx, dy, dz), device_id_type=MESH))
     begin(zcopies, esends)
+    vct[1:1 + depth, 1:1 + height] = vc[...]
+
+    def clear(ref, d0, h0):
+        for d, (dx, dy) in enumerate(DIRS):
+            _, (a, n) = span(dx, d0, 1)
+            _, (b, m) = span(dy, h0, 1)
+
+            def zero(a=a, n=n, b=b, m=m):
+                ref[a:a + n, b:b + m] = jnp.zeros((n, m) + ref.shape[2:], ref.dtype)
+
+            if recvs[d] is not None:
+                pl.when(jnp.logical_not(recvs[d]))(zero)
+
+    for ref in (vct, skip, eh):
+        clear(ref, depth, height)
+    for ref in (ph, uh, gh):
+        clear(ref, cd, ch)
+    for d, (dx, dy, dz) in enumerate(ends):
+        _, (b, m) = span(dx, depth, 1)
+
+        def zero(side=1 if dz > 0 else 0, dyi=1 - dy, b=b, m=m):
+            er[side, dyi, b:b + m] = jnp.zeros((m, chans, width), BF)
+
+        pl.when(jnp.logical_not(erecvs[d]))(zero)
+
     for c in loads:
         c.wait()
     arrange_weights(enc_w, coarse_w, upt, dec_w, we, wd, wdb, wc, wcb, web, up)

time: 65.3 us -> 64.4 us (0.986)
  Pallas kernels: 62.5 us -> 61.6 us
    pallas_call x1, Pallas kernels: 61 us -> 60.1 us  [per_device(): pl.pallas_call(functools.partial(kernel, sizes), out_shape=(jax.ShapeDtyp...]
where the time goes in v7:
time: 64.4 us; the launch traced here: 64.3 us
  Pallas kernels  61.6 us (96%)
  local copies, waits for them, and re-layouts  1.95 us (3%)
  between operations  0.7 us (1%)
    pallas_call x1, Pallas kernels, per_device(): pl.pallas_call(functools.partial(kernel, sizes), out_shape=(jax.ShapeDtyp...  60.1 us
    unnamed x12, local copies, waits for them, and re-layouts  1.95 us
    pallas_call x1, Pallas kernels, per_device(): pl.pallas_call(functools.partial(finish, owners * pers[0]), out_shape=tup...  1.54 us

profile of v7, /device:TPU:1, one launch (start us, length us, event | category | flops | bytes accessed | tf_op | source)
XLA Modules:
  0.0 64.3 jit_solution(14715786971938745280)
XLA Ops:
  0.6 0.0 copy-start.4
  0.6 1.0 %copy.12 = bf16[16,4,8,128]{3,0,2,1:T(8,128)(2,1)S(1)} copy(bf16[16,4,8,128]{3,2,1,0:T(8,128)(2,1)} %param.6) | data formatting | bytes 262144 | tf_op args[0]
  1.6 0.0 copy-done.4
  1.6 0.1 copy.13
  1.7 0.0 copy-start
  1.7 0.0 copy-start.1
  1.7 0.0 copy-start.2
  1.7 0.0 copy-start.3
  1.8 0.8 %copy-done = bf16[27,16,32]{2,1,0:T(8,128)(2,1)S(1)} copy-done((bf16[27,16,32]{2,1,0:T(8,128)(2,1)S(1)}, bf16[27,16,32]{2,1,0:T(8,128)(2,1)}, u32[]{:S(2)}) %copy-start) | copy-done | bytes 27672
  2.6 0.1 copy-done.1
  2.7 0.0 copy-done.2
  2.7 0.0 copy-done.3
  2.7 60.1 %shard_map.109 = (bf16[16,4,8,128]{3,2,1,0:T(8,128)(2,1)S(1)}, bf16[16,4,8,128]{3,2,1,0:T(8,128)(2,1)S(1)}, bf16[24,16,128]{2,1,0:T(8,128)(2,1)S(1)}) custom-call(bf16[4,8,32,128]{3,2,1,0:T(8,128)(2,1)S(1)} %maximum_bitcast_fusion.vc, bf16[16,16,27]{2,1,0:T(8,128)(2,1)S(1)} %bitcast.9, bf16[27,16,32]{2,1,0:T(8,128)(2,1)S(1)} %copy-done, ...), custom_call_target="tpu_custom_call" | custom-call | tf_op jit(solution)/shard_map/pallas_call | solution.py:680
  62.7 1.5 %shard_map.110 = (bf16[16,4,8,128]{3,2,1,0:T(8,128)(2,1)}, bf16[16,4,8,128]{3,2,1,0:T(8,128)(2,1)}, f32[16,16,27]{2,1,0:T(8,128)}, f32[27,16,32]{2,1,0:T(8,128)}...) custom-call(bf16[16,4,8,128]{3,2,1,0:T(8,128)(2,1)S(1)} %get-tuple-element.15.dec, ...), custom_call_target="tpu_custom_call" | custom-call | tf_op jit(solution)/shard_map/pallas_call | solution.py:693
  (1 shorter events, 0.0 us)
Async XLA Ops:
  0.6 1.0 %copy-start.4 = (bf16[16,4,8,128]{3,2,1,0:T(8,128)(2,1)S(1)}, bf16[16,4,8,128]{3,2,1,0:T(8,128)(2,1)}, u32[]{:S(2)}) copy-start(bf16[16,4,8,128]{3,2,1,0:T(8,128)(2,1)} %param.11) | copy-start | bytes 393220
  1.7 0.9 %copy-start = (bf16[27,16,32]{2,1,0:T(8,128)(2,1)S(1)}, bf16[27,16,32]{2,1,0:T(8,128)(2,1)}, u32[]{:S(2)}) copy-start(bf16[27,16,32]{2,1,0:T(8,128)(2,1)} %coarse_in.1) | copy-start | bytes 82948
  1.7 0.9 %copy-start.1 = (bf16[27,32,16]{1,2,0:T(8,128)(2,1)S(1)}, bf16[27,32,16]{1,2,0:T(8,128)(2,1)}, u32[]{:S(2)}) copy-start(bf16[27,32,16]{1,2,0:T(8,128)(2,1)} %param.10) | copy-start | bytes 82948
  1.7 0.9 %copy-start.2 = (bf16[27,16,16]{0,2,1:T(8,128)(2,1)S(1)}, bf16[27,16,16]{0,2,1:T(8,128)(2,1)}, u32[]{:S(2)}) copy-start(bf16[27,16,16]{0,2,1:T(8,128)(2,1)} %param.7) | copy-start | bytes 41476
  1.7 0.9 %copy-start.3 = (bf16[32,16]{0,1:T(8,128)(2,1)S(1)}, bf16[32,16]{0,1:T(8,128)(2,1)}, u32[]{:S(2)}) copy-start(bf16[32,16]{0,1:T(8,128)(2,1)} %param.9) | copy-start | bytes 3076

commit v8 on v7

--- a/solution.py
+++ b/solution.py
@@ -545,7 +545,6 @@
         back_row(q, None)
     ecopies = exchange(eh, rim_src(1, depth, height, 1), eh, rim_dst(1, depth, height), esend, erecv)
     begin(ecopies, sends)
-    early = advance(0, early, 0)
 
     landed(ucopies, recvs)
     low = lax.broadcasted_iota(jnp.int32, (width, width), 0)
@@ -569,6 +568,7 @@
     put(gr1, 6, place(side, group16, 0, last))
 
     late = ring(1, 0)
+    early = advance(0, early, 0)
 
     order = zero_one((height * chans, height * chans),
                      lambda r, l: (r // height == l % chans) & (r % height == l // chans)).astype(BF)

time: 64.4 us -> 64.4 us (level)
  no operation moved by 1% of the time
where the time goes in v8:
time: 64.4 us; the launch traced here: 64.2 us
  Pallas kernels  61.5 us (95%)
  local copies, waits for them, and re-layouts  1.95 us (3%)
  between operations  0.7 us (1%)
    pallas_call x1, Pallas kernels, per_device(): pl.pallas_call(functools.partial(kernel, sizes), out_shape=(jax.ShapeDtyp...  60 us
    unnamed x12, local copies, waits for them, and re-layouts  1.95 us
    pallas_call x1, Pallas kernels, per_device(): pl.pallas_call(functools.partial(finish, owners * pers[0]), out_shape=tup...  1.54 us

profile of v8, /device:TPU:1, one launch (start us, length us, event | category | flops | bytes accessed | tf_op | source)
XLA Modules:
  0.0 64.2 jit_solution(1090685942195224422)
XLA Ops:
  0.6 0.0 copy-start.4
  0.6 1.0 %copy.12 = bf16[16,4,8,128]{3,0,2,1:T(8,128)(2,1)S(1)} copy(bf16[16,4,8,128]{3,2,1,0:T(8,128)(2,1)} %param.6) | data formatting | bytes 262144 | tf_op args[0]
  1.6 0.0 copy-done.4
  1.6 0.1 copy.13
  1.7 0.0 copy-start
  1.7 0.0 copy-start.1
  1.7 0.0 copy-start.2
  1.7 0.0 copy-start.3
  1.8 0.8 %copy-done = bf16[27,16,32]{2,1,0:T(8,128)(2,1)S(1)} copy-done((bf16[27,16,32]{2,1,0:T(8,128)(2,1)S(1)}, bf16[27,16,32]{2,1,0:T(8,128)(2,1)}, u32[]{:S(2)}) %copy-start) | copy-done | bytes 27672
  2.6 0.1 copy-done.1
  2.7 0.0 copy-done.2
  2.7 0.0 copy-done.3
  2.7 60.0 %shard_map.109 = (bf16[16,4,8,128]{3,2,1,0:T(8,128)(2,1)S(1)}, bf16[16,4,8,128]{3,2,1,0:T(8,128)(2,1)S(1)}, bf16[24,16,128]{2,1,0:T(8,128)(2,1)S(1)}) custom-call(bf16[4,8,32,128]{3,2,1,0:T(8,128)(2,1)S(1)} %maximum_bitcast_fusion.vc, bf16[16,16,27]{2,1,0:T(8,128)(2,1)S(1)} %bitcast.9, bf16[27,16,32]{2,1,0:T(8,128)(2,1)S(1)} %copy-done, ...), custom_call_target="tpu_custom_call" | custom-call | tf_op jit(solution)/shard_map/pallas_call | solution.py:680
  62.7 1.5 %shard_map.110 = (bf16[16,4,8,128]{3,2,1,0:T(8,128)(2,1)}, bf16[16,4,8,128]{3,2,1,0:T(8,128)(2,1)}, f32[16,16,27]{2,1,0:T(8,128)}, f32[27,16,32]{2,1,0:T(8,128)}...) custom-call(bf16[16,4,8,128]{3,2,1,0:T(8,128)(2,1)S(1)} %get-tuple-element.15.dec, ...), custom_call_target="tpu_custom_call" | custom-call | tf_op jit(solution)/shard_map/pallas_call | solution.py:693
  (1 shorter events, 0.0 us)
Async XLA Ops:
  0.6 1.0 %copy-start.4 = (bf16[16,4,8,128]{3,2,1,0:T(8,128)(2,1)S(1)}, bf16[16,4,8,128]{3,2,1,0:T(8,128)(2,1)}, u32[]{:S(2)}) copy-start(bf16[16,4,8,128]{3,2,1,0:T(8,128)(2,1)} %param.11) | copy-start | bytes 393220
  1.7 0.9 %copy-start = (bf16[27,16,32]{2,1,0:T(8,128)(2,1)S(1)}, bf16[27,16,32]{2,1,0:T(8,128)(2,1)}, u32[]{:S(2)}) copy-start(bf16[27,16,32]{2,1,0:T(8,128)(2,1)} %coarse_in.1) | copy-start | bytes 82948
  1.7 0.9 %copy-start.1 = (bf16[27,32,16]{1,2,0:T(8,128)(2,1)S(1)}, bf16[27,32,16]{1,2,0:T(8,128)(2,1)}, u32[]{:S(2)}) copy-start(bf16[27,32,16]{1,2,0:T(8,128)(2,1)} %param.10) | copy-start | bytes 82948
  1.7 0.9 %copy-start.2 = (bf16[27,16,16]{0,2,1:T(8,128)(2,1)S(1)}, bf16[27,16,16]{0,2,1:T(8,128)(2,1)}, u32[]{:S(2)}) copy-start(bf16[27,16,16]{0,2,1:T(8,128)(2,1)} %param.7) | copy-start | bytes 41476
  1.7 0.9 %copy-start.3 = (bf16[32,16]{0,1:T(8,128)(2,1)S(1)}, bf16[32,16]{0,1:T(8,128)(2,1)}, u32[]{:S(2)}) copy-start(bf16[32,16]{0,1:T(8,128)(2,1)} %param.9) | copy-start | bytes 3076

commit v9 on v8

--- a/solution.py
+++ b/solution.py
@@ -544,7 +544,6 @@
     for q in (0, ch - 1):
         back_row(q, None)
     ecopies = exchange(eh, rim_src(1, depth, height, 1), eh, rim_dst(1, depth, height), esend, erecv)
-    begin(ecopies, sends)
 
     landed(ucopies, recvs)
     low = lax.broadcasted_iota(jnp.int32, (width, width), 0)
@@ -568,6 +567,7 @@
     put(gr1, 6, place(side, group16, 0, last))
 
     late = ring(1, 0)
+    begin(ecopies, sends)
     early = advance(0, early, 0)
 
     order = zero_one((height * chans, height * chans),

time: 64.4 us -> 64.9 us (level)
  no operation moved by 1% of the time
where the time goes in v9:
time: 64.9 us; the launch traced here: 64.7 us
  Pallas kernels  62.1 us (96%)
  local copies, waits for them, and re-layouts  1.95 us (3%)
  between operations  0.7 us (1%)
    pallas_call x1, Pallas kernels, per_device(): pl.pallas_call(functools.partial(kernel, sizes), out_shape=(jax.ShapeDtyp...  60.5 us
    unnamed x12, local copies, waits for them, and re-layouts  1.95 us
    pallas_call x1, Pallas kernels, per_device(): pl.pallas_call(functools.partial(finish, owners * pers[0]), out_shape=tup...  1.54 us

profile of v9, /device:TPU:1, one launch (start us, length us, event | category | flops | bytes accessed | tf_op | source)
XLA Modules:
  0.0 64.7 jit_solution(11361546244231921265)
XLA Ops:
  0.6 0.0 copy-start.4
  0.6 1.0 %copy.12 = bf16[16,4,8,128]{3,0,2,1:T(8,128)(2,1)S(1)} copy(bf16[16,4,8,128]{3,2,1,0:T(8,128)(2,1)} %param.6) | data formatting | bytes 262144 | tf_op args[0]
  1.6 0.0 copy-done.4
  1.6 0.1 copy.13
  1.7 0.0 copy-start
  1.7 0.0 copy-start.1
  1.7 0.0 copy-start.2
  1.7 0.0 copy-start.3
  1.8 0.8 %copy-done = bf16[27,16,32]{2,1,0:T(8,128)(2,1)S(1)} copy-done((bf16[27,16,32]{2,1,0:T(8,128)(2,1)S(1)}, bf16[27,16,32]{2,1,0:T(8,128)(2,1)}, u32[]{:S(2)}) %copy-start) | copy-done | bytes 27672
  2.6 0.1 copy-done.1
  2.7 0.0 copy-done.2
  2.7 0.0 copy-done.3
  2.7 60.5 %shard_map.109 = (bf16[16,4,8,128]{3,2,1,0:T(8,128)(2,1)S(1)}, bf16[16,4,8,128]{3,2,1,0:T(8,128)(2,1)S(1)}, bf16[24,16,128]{2,1,0:T(8,128)(2,1)S(1)}) custom-call(bf16[4,8,32,128]{3,2,1,0:T(8,128)(2,1)S(1)} %maximum_bitcast_fusion.vc, bf16[16,16,27]{2,1,0:T(8,128)(2,1)S(1)} %bitcast.9, bf16[27,16,32]{2,1,0:T(8,128)(2,1)S(1)} %copy-done, ...), custom_call_target="tpu_custom_call" | custom-call | tf_op jit(solution)/shard_map/pallas_call | solution.py:680
  63.2 1.5 %shard_map.110 = (bf16[16,4,8,128]{3,2,1,0:T(8,128)(2,1)}, bf16[16,4,8,128]{3,2,1,0:T(8,128)(2,1)}, f32[16,16,27]{2,1,0:T(8,128)}, f32[27,16,32]{2,1,0:T(8,128)}...) custom-call(bf16[16,4,8,128]{3,2,1,0:T(8,128)(2,1)S(1)} %get-tuple-element.15.dec, ...), custom_call_target="tpu_custom_call" | custom-call | tf_op jit(solution)/shard_map/pallas_call | solution.py:693
  (1 shorter events, 0.0 us)
Async XLA Ops:
  0.6 1.0 %copy-start.4 = (bf16[16,4,8,128]{3,2,1,0:T(8,128)(2,1)S(1)}, bf16[16,4,8,128]{3,2,1,0:T(8,128)(2,1)}, u32[]{:S(2)}) copy-start(bf16[16,4,8,128]{3,2,1,0:T(8,128)(2,1)} %param.11) | copy-start | bytes 393220
  1.7 0.9 %copy-start = (bf16[27,16,32]{2,1,0:T(8,128)(2,1)S(1)}, bf16[27,16,32]{2,1,0:T(8,128)(2,1)}, u32[]{:S(2)}) copy-start(bf16[27,16,32]{2,1,0:T(8,128)(2,1)} %coarse_in.1) | copy-start | bytes 82948
  1.7 0.9 %copy-start.1 = (bf16[27,32,16]{1,2,0:T(8,128)(2,1)S(1)}, bf16[27,32,16]{1,2,0:T(8,128)(2,1)}, u32[]{:S(2)}) copy-start(bf16[27,32,16]{1,2,0:T(8,128)(2,1)} %param.10) | copy-start | bytes 82948
  1.7 0.9 %copy-start.2 = (bf16[27,16,16]{0,2,1:T(8,128)(2,1)S(1)}, bf16[27,16,16]{0,2,1:T(8,128)(2,1)}, u32[]{:S(2)}) copy-start(bf16[27,16,16]{0,2,1:T(8,128)(2,1)} %param.7) | copy-start | bytes 41476
  1.7 0.9 %copy-start.3 = (bf16[32,16]{0,1:T(8,128)(2,1)S(1)}, bf16[32,16]{0,1:T(8,128)(2,1)}, u32[]{:S(2)}) copy-start(bf16[32,16]{0,1:T(8,128)(2,1)} %param.9) | copy-start | bytes 3076
